TPU v7x, 128 devices: a whole 4x4x4 slice. The times are simulated.
128 devices in a mesh: row: 8 (over x, core), col: 16 (over z, y).
Axes of the slice: x: 4, y: 4, z: 4, core: 2. Of those that a mesh axis runs over, the one named last changes fastest.
Arguments:
- coords: float32 [4, 16384], P(None, ('row', 'col')), may hold values from 0 to 1, as said below
- values: float32 [512, 16384], P(None, ('row', 'col')), may hold values from -6 to 6
- coarse_coords: float32 [4, 2048], P(None, ('row', 'col')), may hold values from 0 to 1, as said below
- coarse_values: float32 [512, 2048], P(None, ('row', 'col')), may hold values from -6 to 6
- fine_index: int32 [128, 128], P(('row', 'col')), may hold values from 0 to 127, as said below
- coarse_index: int32 [128, 384], P(('row', 'col')), may hold values from 0 to 2047, as said below
- log_params: float32 [6], replicated, may hold values from -0.5 to 0.5
Outputs:
- step: float32 [6], replicated
- whitened: float32 [512, 16384], P(None, ('row', 'col'))
Inputs may be any that keep to these rules, and one draw needn't show every extreme that they name: `fine_index`: in each row the first 64 entries are distinct, and so are the last 64. `coarse_index`: the entries of each row are distinct; in each row at most 6 entries lie in one tile (j // 16), and some tile holds exactly 6 of them. `coarse_coords`: coarse point j lies in tile j // 16; for tile (r, c) its longitude lies in [c / 16, (c + 1) / 16) and its latitude in [r / 8, (r + 1) / 8), elevation and time in [0, 1). `coords`: fine point p lies in tile p // 128, placed as for the coarse points.
All inputs are finite; a program needn't handle non-finite values.
Results may differ from a plain program's by a relative error of at most 0.0003.
Values sent between devices are 32-bit elements; how exact they have to be, the bound alone decides.
No kernel may reach another device: no remote copies, remote signals or barrier semaphores. Data moves between devices by JAX's collectives and lax.ppermute only.
A program may use at most 192 MiB of HBM per device.

v0:
```python
import math

import jax
import jax.numpy as jnp
from jax import lax
from jax.sharding import PartitionSpec as P

HIGH = lax.Precision.HIGHEST
ROOT_FIVE = math.sqrt(5.0)
NUGGET = 0.2
RANGE_BASE = (0.5, 0.5, 0.5, 0.5)


def shifted(value, axis, steps):
    count = lax.axis_size(axis)
    first, last = (max(0, -steps), min(count, count - steps))
    return lax.ppermute(value, axis, [(source, source + steps) for source in range(first, last)])


def passed_along(block, axis, distance):
    devices = range(lax.axis_size(axis))
    route = [((i - distance) % len(devices), i) for i in devices]
    return lax.ppermute(block, axis, route)


def local_covariance(joint_coords, live, theta):
    count = joint_coords.shape[1]
    scale = jnp.exp(theta[1:5]) * jnp.array(RANGE_BASE)
    scaled = joint_coords / scale[:, None]
    diff = scaled[:, :, None] - scaled[:, None, :]
    squares = diff * diff
    dist = jnp.sqrt(jnp.sum(squares, axis=0))
    root = ROOT_FIVE * dist
    decay = jnp.exp(-root)
    variance = jnp.exp(theta[0])
    kernel = variance * (1.0 + root + root * root / 3.0) * decay
    common = variance * (5.0 / 3.0) * (1.0 + root) * decay
    paired = live[:, None] * live[None, :]
    ident = jnp.eye(count, dtype=jnp.float32)
    nugget = NUGGET * jnp.exp(theta[5])
    cov = paired * kernel + (live * nugget + 1.0 - live)[:, None] * ident
    derivs = jnp.concatenate(
        [
            (paired * kernel)[None],
            (paired * common)[None] * squares,
            ((live * nugget)[:, None] * ident)[None],
        ],
        axis=0,
    )
    return (cov, derivs)


def fisher_terms(cov, derivs, lead, reps):
    count = cov.shape[0]
    ident = jnp.eye(count, dtype=jnp.float32)
    factor = jnp.linalg.cholesky(cov)
    inverse = jax.scipy.linalg.solve_triangular(factor, ident, lower=True)
    joint_prec = jnp.dot(inverse.T, inverse, precision=HIGH)
    lead_inv = inverse[:lead, :lead]
    lead_prec = jnp.dot(lead_inv.T, lead_inv, precision=HIGH)
    joint_prod = jnp.einsum("ab,ibc->iac", joint_prec, derivs, precision=HIGH)
    lead_prod = jnp.einsum("ab,ibc->iac", lead_prec, derivs[:, :lead, :lead], precision=HIGH)
    joint_fish = jnp.einsum("iab,jba->ij", joint_prod, joint_prod, precision=HIGH)
    lead_fish = jnp.einsum("iab,jba->ij", lead_prod, lead_prod, precision=HIGH)
    fisher = reps * 0.5 * (joint_fish - lead_fish)
    traces = jnp.trace(joint_prod, axis1=1, axis2=2) - jnp.trace(lead_prod, axis1=1, axis2=2)
    return (inverse, fisher, traces)


def score_terms(inverse, derivs, joint_values, traces, lead, reps):
    white = jnp.dot(joint_values, inverse.T, precision=HIGH)
    alpha = jnp.dot(white, inverse, precision=HIGH)
    lead_alpha = jnp.dot(white[:, :lead], inverse[:lead, :lead], precision=HIGH)
    joint_quad = jnp.sum(
        jnp.einsum("rn,inm->irm", alpha, derivs, precision=HIGH) * alpha[None], axis=(1, 2)
    )
    lead_quad = jnp.sum(
        jnp.einsum("rn,inm->irm", lead_alpha, derivs[:, :lead, :lead], precision=HIGH)
        * lead_alpha[None],
        axis=(1, 2),
    )
    grad = 0.5 * (joint_quad - lead_quad) - 0.5 * reps * traces
    return (grad, white[:, lead:])


def body(coords, values, coarse_coords, coarse_values, fine_index, coarse_index, log_params):
    half = fine_index.shape[1] // 2
    reps = values.shape[0]
    block_size = coords.shape[1]
    pick_upper = fine_index[0, :half]
    pick_left = fine_index[0, half:]
    wanted = coarse_index[0]
    num_coarse = wanted.shape[0]
    lead = num_coarse + 2 * half
    upper_coords, upper_values = shifted((coords, values), "row", 1)
    left_coords, left_values = passed_along((coords, values), "col", 1)
    upper_coords = jnp.take(upper_coords, pick_upper, axis=1)
    upper_values = jnp.take(upper_values, pick_upper, axis=1)
    left_coords = jnp.take(left_coords, pick_left, axis=1)
    left_values = jnp.take(left_values, pick_left, axis=1)
    every_coords, every_values = (
        lax.all_gather(coarse_coords, ("row", "col"), axis=1, tiled=True),
        lax.all_gather(coarse_values, ("row", "col"), axis=1, tiled=True),
    )
    picked_coords = jnp.take(every_coords, wanted, axis=1)
    picked_values = jnp.take(every_values, wanted, axis=1)
    upper_live = (lax.axis_index("row") > 0).astype(jnp.float32)
    joint_coords = jnp.concatenate([picked_coords, upper_coords, left_coords, coords], axis=1)
    joint_values = jnp.concatenate([picked_values, upper_values, left_values, values], axis=1)
    live = jnp.concatenate(
        [
            jnp.ones((num_coarse,), jnp.float32),
            upper_live * jnp.ones((half,), jnp.float32),
            jnp.ones((half + block_size,), jnp.float32),
        ]
    )
    cov, derivs = local_covariance(joint_coords, live, log_params)
    inverse, fisher, traces = fisher_terms(cov, derivs, lead, reps)
    grad, white = score_terms(inverse, derivs, joint_values, traces, lead, reps)
    grad, fisher = lax.psum((grad, fisher), ("row", "col"))
    step = jax.scipy.linalg.cho_solve((jnp.linalg.cholesky(fisher), True), grad)
    return (step, white)


def solution(mesh):
    in_specs = (
        P(None, ("row", "col")),
        P(None, ("row", "col")),
        P(None, ("row", "col")),
        P(None, ("row", "col")),
        P(("row", "col"), None),
        P(("row", "col"), None),
        P(),
    )
    out_specs = (P(), P(None, ("row", "col")))
    return jax.shard_map(body, mesh=mesh, in_specs=in_specs, out_specs=out_specs, check_vma=False)
```

profile of v0, /device:TPU:1, one launch (start us, length us, event | category | flops | bytes accessed | tf_op | source)
XLA Modules:
  0.0 621.7 jit_solution(13361422964512094630)
XLA Ops:
  24.7 58.2 %all-gather = f32[128,16,4]{1,2,0:T(4,128)S(1)} all-gather(f32[1,16,4]{1,2,0:T(4,128)S(1)} %bitcast.159), channel_id=1, replica_groups=mesh['row'=8,'col'=16] {'row','col'}, dimensions={0}, use_global_device_ids=true | all-gather | bytes 33024 | tf_op jit(solution)/shard_map/all_gather | solution.py:102
  109.5 13.2 %cholesky.146 = f32[128,128]{1,0:T(8,128)} custom-call(f32[128,128]{1,0:T(8,128)} %cholesky.372), custom_call_target="Cholesky" | custom-call | tf_op jit(solution)/shard_map/jit(cholesky)/cholesky | solution.py:56
  126.8 11.3 %custom-call.49 = f32[1,128,128]{1,2,0:T(8,128)} custom-call(f32[1,128,128]{2,1,0:T(8,128)} %get-tuple-element.43), custom_call_target="InvertDiagBlocksLowerTriangular" | custom-call | tf_op jit(solution)/shard_map/jit(cholesky)/cholesky | solution.py:56
  142.9 13.2 %cholesky.171 = f32[128,128]{1,0:T(8,128)} custom-call(f32[128,128]{1,0:T(8,128)} %cholesky.376), custom_call_target="Cholesky" | custom-call | tf_op jit(solution)/shard_map/jit(cholesky)/cholesky | solution.py:56
  158.0 11.5 %custom-call.50 = f32[1,128,128]{1,2,0:T(8,128)} custom-call(f32[1,128,128]{2,1,0:T(8,128)} %get-tuple-element.40), custom_call_target="InvertDiagBlocksLowerTriangular" | custom-call | tf_op jit(solution)/shard_map/jit(cholesky)/cholesky | solution.py:56
  174.4 13.2 %cholesky.317 = f32[128,128]{1,0:T(8,128)} custom-call(f32[128,128]{1,0:T(8,128)} %cholesky.381), custom_call_target="Cholesky" | custom-call | tf_op jit(solution)/shard_map/jit(cholesky)/cholesky | solution.py:56
  189.6 11.3 %custom-call.51 = f32[1,128,128]{1,2,0:T(8,128)} custom-call(f32[1,128,128]{2,1,0:T(8,128)} %get-tuple-element.37), custom_call_target="InvertDiagBlocksLowerTriangular" | custom-call | tf_op jit(solution)/shard_map/jit(cholesky)/cholesky | solution.py:56
  205.6 13.5 %cholesky.336 = f32[128,128]{1,0:T(8,128)} custom-call(f32[128,128]{1,0:T(8,128)} %cholesky.386), custom_call_target="Cholesky" | custom-call | tf_op jit(solution)/shard_map/jit(cholesky)/cholesky | solution.py:56
  221.2 11.3 %custom-call.52 = f32[1,128,128]{1,2,0:T(8,128)} custom-call(f32[1,128,128]{2,1,0:T(8,128)} %get-tuple-element.34), custom_call_target="InvertDiagBlocksLowerTriangular" | custom-call | tf_op jit(solution)/shard_map/jit(cholesky)/cholesky | solution.py:56
  236.2 13.2 %cholesky.353 = f32[128,128]{1,0:T(8,128)} custom-call(f32[128,128]{1,0:T(8,128)} %convolution_subtract_fusion.6), custom_call_target="Cholesky" | custom-call | tf_op jit(solution)/shard_map/jit(cholesky)/cholesky | solution.py:56
  262.1 20.9 %while.1 = (s32[]{:T(128)}, f32[640,640]{1,0:T(8,128)}, s32[5,2]{0,1:T(2,128)}, f32[5,128,128]{2,1,0:T(8,128)}, s32[]{:T(128)}) while((s32[]{:T(128)}, f32[640,640]{1,0:T(8,128)}, s32[5,2]{0,1:T(2,128)}, f32[5,128,128]{2,1,0:T(8,128)}, s32[]{:T(128)}) %tuple.51), condition=%wide.while_cond, body=%wide.while_body.sunk | while | flops 2 | bytes 132205 | solution.py:57
  282.9 50.6 %custom-call.53 = f32[5,128,128]{1,2,0:T(8,128)} custom-call(f32[5,128,128]{2,1,0:T(8,128)} %get-tuple-element.11), custom_call_target="InvertDiagBlocksLowerTriangular" | custom-call | tf_op jit(solution)/shard_map/jit(_solve_triangular)/triangular_solve | solution.py:57
  349.6 5.1 fusion.99
  356.7 29.3 %select_reduce_fusion = (f32[6]{0:T(128)S(1)}, f32[6,640,640]{1,2,0:T(8,128)}) fusion(pred[640,640]{0,1:T(8,128)(4,1)S(1)} %copy-done.22, f32[640,640]{1,0:T(8,128)S(1)} %fusion.99, f32[1,640,640]{1,2,0:T(8,128)S(1)} %copy-done.5, f32[4,640,640]{1,2,0:T(8,128)S(1)} %fusion.7, f32[1,640,640]{1,2,0:T(8,128)S(1)} %copy-done.7), kind=kOutput, calls=%fused_computation.11 | convolution fusion | flops 18884198400 | bytes 21708824 | tf_op jit(solution)/shard_map/ab,ibc->iac/dot_general | solution.py:61
  386.0 14.3 %copy.71 = f32[6,640,640]{2,0,1:T(8,128)} copy(f32[6,640,640]{1,2,0:T(8,128)} %get-tuple-element.63) | data formatting | bytes 19660800 | tf_op jit(solution)/shard_map/ab,ibc->iac/transpose | solution.py:61
  402.3 16.1 %select_reduce_fusion.1 = (f32[6]{0:T(128)S(1)}, f32[6,512,512]{1,2,0:T(8,128)}) fusion(pred[512,512]{0,1:T(8,128)(4,1)S(1)} %copy-done.18, f32[512,512,1]{1,0,2:T(8,128)S(1)} %convolution_bitcast_fusion.1, f32[1,640,640]{1,2,0:T(8,128)S(1)} %copy-done.5, f32[4,640,640]{1,2,0:T(8,128)} %copy-done.3, f32[1,640,640]{1,2,0:T(8,128)S(1)} %copy-done.8), kind=kOutput, calls=%fused_computation.24 | convolution fusion | flops 9669967872 | bytes 17432600 | tf_op jit(solution)/shard_map/ab,ibc->iac/dot_general | solution.py:62
  418.4 9.8 %copy.73 = f32[6,512,512]{2,0,1:T(8,128)} copy(f32[6,512,512]{1,2,0:T(8,128)} %get-tuple-element.65) | data formatting | bytes 12582912 | tf_op jit(solution)/shard_map/ab,ibc->iac/transpose | solution.py:62
  428.1 34.7 %fusion.36 = f32[6,6]{0,1:T(8,128)S(1)} fusion(f32[6,640,640]{2,0,1:T(8,128)} %copy.71, f32[6,640,640]{1,2,0:T(8,128)} %get-tuple-element.63), kind=kOutput, calls=%fused_computation.72 | convolution fusion | flops 176947200 | bytes 19660944 | tf_op jit(solution)/shard_map/iab,jba->ij/dot_general | solution.py:63
  462.9 18.9 %fusion.42 = f32[6,6]{0,1:T(8,128)S(1)} fusion(f32[6,6]{0,1:T(8,128)S(1)} %fusion.36, f32[6,512,512]{2,0,1:T(8,128)S(1)} %copy-done, f32[6,512,512]{1,2,0:T(8,128)S(1)} %bitcast.157), kind=kOutput, calls=%fused_computation.74 | convolution fusion | flops 113246280 | bytes 12583200 | tf_op jit(solution)/shard_map/iab,jba->ij/dot_general | solution.py:64
  489.5 7.4 %fusion.21 = f32[512,640]{1,0:T(8,128)S(1)} fusion(f32[640,640]{1,0:T(8,128)S(1)} %copy-done.2, f32[512,128]{0,1:T(8,128)} %copy.79, f32[512,64]{0,1:T(8,128)S(1)} %select_bitcast_fusion.2, f32[512,64]{0,1:T(8,128)S(1)} %select_bitcast_fusion.3, f32[512,384]{0,1:T(8,128)S(1)} %select_bitcast_fusion), kind=kOutput, calls=%fused_computation.50 | convolution fusion | flops 2517565440 | bytes 4259840 | tf_op jit(solution)/shard_map/dot_general | solution.py:71
  496.9 4.8 fusion.100
  507.7 21.7 %fusion.4 = f32[6]{0:T(128)S(1)} fusion(f32[512,640]{0,1:T(8,128)} %copy.82, f32[1,640,640]{1,2,0:T(8,128)S(1)} %copy-done.6, f32[4,640,640]{1,2,0:T(8,128)} %copy-done.3, f32[1,640,640]{1,2,0:T(8,128)} %copy.68, f32[512,640]{1,0:T(8,128)} %fusion.100), kind=kOutput, calls=%fused_computation.15 | convolution fusion | flops 15108341760 | bytes 12451864 | tf_op jit(solution)/shard_map/rn,inm->irm/dot_general | solution.py:75
  532.0 13.8 %fusion.9 = f32[6]{0:T(128)S(1)} fusion(f32[512,512]{0,1:T(8,128)} %copy.83, f32[1,640,640]{1,2,0:T(8,128)S(1)} %copy-done.6, f32[4,640,640]{1,2,0:T(8,128)} %copy-done.3, f32[1,640,640]{1,2,0:T(8,128)} %copy.68, f32[512,512]{1,0:T(8,128)} %fusion.45), kind=kOutput, calls=%fused_computation.23 | convolution fusion | flops 9669967872 | bytes 11927576 | tf_op jit(solution)/shard_map/rn,inm->irm/dot_general | solution.py:78
  546.5 64.6 %all-reduce.1 = (f32[6,6]{0,1:T(8,128)S(1)}, f32[6]{0:T(128)S(1)}) all-reduce(f32[6,6]{0,1:T(8,128)S(1)} %fusion.42, f32[6]{0:T(128)S(1)} %multiply_subtract_fusion), channel_id=1, replica_groups=mesh['row'=8,'col'=16] {'row','col'}, use_global_device_ids=true, to_apply=%region_11.13 | all-reduce | flops 42 | bytes 336 | tf_op jit(solution)/shard_map/psum | solution.py:120
  (207 shorter events, 140.9 us)
Async XLA Ops:
  7.2 16.6 %copy-start.29 = (s32[1,384]{1,0:T(1,128)S(1)}, s32[1,384]{1,0:T(1,128)}, u32[]{:S(2)}) copy-start(s32[1,384]{1,0:T(1,128)} %param.17) | copy-start | bytes 4612
  7.2 17.3 %copy-start.37 = (s32[1,128]{1,0:T(1,128)S(1)}, s32[1,128]{1,0:T(1,128)}, u32[]{:S(2)}) copy-start(s32[1,128]{1,0:T(1,128)} %param.16) | copy-start | bytes 1540
  7.2 17.5 %copy-start.36 = (f32[4,16]{1,0:T(4,128)S(1)}, f32[4,16]{1,0:T(4,128)}, u32[]{:S(2)}) copy-start(f32[4,16]{1,0:T(4,128)} %param.14) | copy-start | bytes 772
  7.2 477.5 %all-gather.3.cloned.1.call-start = ((), (), s32[]{:S(2)}) async-start(), calls=%async_computation | async-start | bytes 4227072 | tf_op jit(solution)/shard_map/all_gather | solution.py:103
  8.0 81.5 %collective-permute-start.1 = (f32[4,128]{0,1:T(8,128)S(1)}, f32[4,128]{0,1:T(8,128)S(1)}, u32[]{:S(2)}, u32[]{:S(2)}) collective-permute-start(f32[4,128]{0,1:T(8,128)S(1)} %copy.61), channel_id=1, source_target_pairs={{15,0},{0,1},{1,2},{2,3},{3,4},{4,5},{5,6},{6,7},{7,8},{8,9},{9,10... | collective-permute-start | bytes 6152 | tf_op jit(solution)/shard_map/ppermute | solution.py:23
  10.2 80.1 %collective-permute-start = (f32[4,128]{0,1:T(8,128)S(1)}, f32[4,128]{0,1:T(8,128)S(1)}, u32[]{:S(2)}, u32[]{:S(2)}) collective-permute-start(f32[4,128]{0,1:T(8,128)S(1)} %copy.61), channel_id=1, source_target_pairs={{0,16},{16,32},{32,48},{48,64},{64,80},{80,96},{96,112},{1,17},{17... | collective-permute-start | bytes 6152 | tf_op jit(solution)/shard_map/ppermute | solution.py:17
  16.0 465.9 %collective-permute-start.3 = (f32[512,128]{0,1:T(8,128)}, f32[512,128]{0,1:T(8,128)}, u32[]{:S(2)}, u32[]{:S(2)}) collective-permute-start(f32[512,128]{0,1:T(8,128)} %copy.79), channel_id=1, source_target_pairs={{15,0},{0,1},{1,2},{2,3},{3,4},{4,5},{5,6},{6,7},{7,8},{8,9},{9,10... | collective-permute-start | bytes 786440 | tf_op jit(solution)/shard_map/ppermute | solution.py:23
  17.3 466.4 %collective-permute-start.2 = (f32[512,128]{0,1:T(8,128)}, f32[512,128]{0,1:T(8,128)S(1)}, u32[]{:S(2)}, u32[]{:S(2)}) collective-permute-start(f32[512,128]{0,1:T(8,128)} %copy.79), channel_id=1, source_target_pairs={{0,16},{16,32},{32,48},{48,64},{64,80},{80,96},{96,112},{1,17},{17... | collective-permute-start | bytes 786440 | tf_op jit(solution)/shard_map/ppermute | solution.py:17
  19.6 67.8 %copy-start.15 = (pred[640,640]{1,0:T(32,128)(4,1)}, pred[640,640]{1,0:T(32,128)(4,1)S(1)}, u32[]{:S(2)}) copy-start(pred[640,640]{1,0:T(32,128)(4,1)S(1)} %iota_compare_fusion.1) | copy-start | bytes 1228804
  24.6 65.6 %copy-start.34 = (pred[64]{0:T(512)(128)(4,1)}, pred[64]{0:T(512)(128)(4,1)S(1)}, u32[]{:S(2)}) copy-start(pred[64]{0:T(512)(128)(4,1)S(1)} %get-tuple-element.50) | copy-start | bytes 196
  24.6 66.3 %copy-start.32 = (pred[64]{0:T(512)(128)(4,1)}, pred[64]{0:T(512)(128)(4,1)S(1)}, u32[]{:S(2)}) copy-start(pred[64]{0:T(512)(128)(4,1)S(1)} %get-tuple-element.22) | copy-start | bytes 196
  24.6 64.9 %copy-start.28 = (s32[1024]{0:T(1024)}, s32[1024]{0:T(1024)S(1)}, u32[]{:S(2)}) copy-start(s32[1024]{0:T(1024)S(1)} %pad_clamp_fusion) | copy-start | bytes 12292
  24.6 65.7 %copy-start.27 = (s32[1024]{0:T(1024)}, s32[1024]{0:T(1024)S(1)}, u32[]{:S(2)}) copy-start(s32[1024]{0:T(1024)S(1)} %pad_clamp_fusion.1) | copy-start | bytes 12292
  83.6 6.7 %copy-start.24 = (s32[1024]{0:T(1024)}, s32[1024]{0:T(1024)S(1)}, u32[]{:S(2)}) copy-start(s32[1024]{0:T(1024)S(1)} %pad_clamp_fusion.2) | copy-start | bytes 12292
  83.7 5.9 copy-start.30
  84.4 6.7 %copy-start.26 = (f32[4,128]{1,0:T(4,128)S(1)}, f32[4,128]{1,0:T(4,128)}, u32[]{:S(2)}) copy-start(f32[4,128]{1,0:T(4,128)} %param.12) | copy-start | bytes 6148
  340.9 59.4 %copy-start.9 = (f32[128,640]{1,0:T(8,128)}, f32[128,640]{1,0:T(8,128)S(1)}, u32[]{:S(2)}) copy-start(f32[128,640]{1,0:T(8,128)S(1)} %get-tuple-element.57) | copy-start | bytes 983044
  343.0 57.4 %copy-start.13 = (f32[128,640]{1,0:T(8,128)}, f32[128,640]{1,0:T(8,128)S(1)}, u32[]{:S(2)}) copy-start(f32[128,640]{1,0:T(8,128)S(1)} %get-tuple-element.59) | copy-start | bytes 983044
  346.2 54.2 %copy-start.16 = (f32[128,640]{1,0:T(8,128)}, f32[128,640]{1,0:T(8,128)S(1)}, u32[]{:S(2)}) copy-start(f32[128,640]{1,0:T(8,128)S(1)} %get-tuple-element.61) | copy-start | bytes 983044
  349.6 5.2 copy-start.1
  356.7 29.3 %copy-start.3 = (f32[4,640,640]{1,2,0:T(8,128)}, f32[4,640,640]{1,2,0:T(8,128)S(1)}, u32[]{:S(2)}) copy-start(f32[4,640,640]{1,2,0:T(8,128)S(1)} %fusion.7) | copy-start | bytes 19660804
  418.4 44.5 %slice-start = ((s8[6291456]{0:T(1024)(128)(4,1)}), s8[2097152]{0:T(1024)(128)(4,1)S(1)}, s32[]{:S(2)}) async-start(s8[6291456]{0:T(1024)(128)(4,1)} %bitcast.156), calls=%async_computation.1 | async-start | bytes 4194304
  428.1 34.8 %slice-start.1 = ((s8[6291456]{0:T(1024)(128)(4,1)}), s8[4194304]{0:T(1024)(128)(4,1)S(1)}, s32[]{:S(2)}) async-start(s8[6291456]{0:T(1024)(128)(4,1)} %bitcast.156), calls=%async_computation.2 | async-start | bytes 8388608
  428.1 34.8 %copy-start = (f32[6,512,512]{2,0,1:T(8,128)S(1)}, f32[6,512,512]{2,0,1:T(8,128)}, u32[]{:S(2)}) copy-start(f32[6,512,512]{2,0,1:T(8,128)} %copy.73) | copy-start | bytes 18874372
  (22 other events, 57.2 us)
Sparse Core Ops, SparseCore 0:
  19.6 68.5 all-gather.2
where the time goes:
time: 630 us; the launch traced here: 622 us
  other arithmetic  197 us (31%)
  matrix products  183 us (29%)
  blocking collectives  123 us (20%)
  local copies, waits for them, and re-layouts  88.8 us (14%)
  between operations  19.9 us (3%)
  starting transfers between devices  9.66 us (2%)
    another operation x18, other arithmetic, fisher_terms(): factor = jnp.linalg.cholesky(cov)  126 us
    psum x1, blocking collectives, body(): grad, fisher = lax.psum((grad, fisher), ('row', 'col'))  64.6 us
    all_gather x1, blocking collectives, body(): lax.all_gather(coarse_coords, ('row', 'col'), axis=1, tiled=True)  58.2 us
    another operation x3, other arithmetic, fisher_terms(): inverse = jax.scipy.linalg.solve_triangular(factor, ident, lower=True)  53.8 us
    dot_general x1, matrix products, fisher_terms(): jnp.einsum('iab,jba->ij', joint_prod, joint_prod, precision=HIGH)  34.7 us
    dot_general x1, matrix products, fisher_terms(): joint_prod = jnp.einsum('ab,ibc->iac', joint_prec, derivs, precision=HIGH)  29.3 us
    dot_general x1, matrix products, score_terms(): jnp.einsum('rn,inm->irm', alpha, derivs, precision=HIGH) * alpha[None]  21.7 us
    another operation x15, local copies, waits for them, and re-layouts  20.9 us
  transfers between devices with their start and end apart: 5, of which 0 were waited for; matrix products, arithmetic and copies ran while one was open for 64% of the time, Pallas kernels for 0%

commit v1 on v0

v1 whole, which is shorter than its diff:
```python
import math

import jax
import jax.numpy as jnp
from jax import lax
from jax.experimental import pallas as pl
from jax.experimental.pallas import tpu as pltpu
from jax.sharding import PartitionSpec as P

HIGH = lax.Precision.HIGHEST
ROOT_FIVE = math.sqrt(5.0)
NUGGET = 0.2
RANGE_BASE = 0.5
F32 = jnp.float32
BF16 = jnp.bfloat16
AXES = ("row", "col")

B = 128
N = 640
LEAD = 512
COARSE = 384
HALF = 64
CP = 16
GROUP = 8


def shifted(value, axis, steps):
    count = lax.axis_size(axis)
    first, last = (max(0, -steps), min(count, count - steps))
    return lax.ppermute(value, axis, [(source, source + steps) for source in range(first, last)])


def passed_along(block, axis, distance):
    devices = range(lax.axis_size(axis))
    route = [((i - distance) % len(devices), i) for i in devices]
    return lax.ppermute(block, axis, route)


def nn(a, b, precision=HIGH):
    return lax.dot_general(a, b, (((1,), (0,)), ((), ())), precision=precision, preferred_element_type=F32)


def nt(a, b, precision=HIGH):
    return lax.dot_general(a, b, (((1,), (1,)), ((), ())), precision=precision, preferred_element_type=F32)


def tn(a, b, precision=HIGH):
    return lax.dot_general(a, b, (((0,), (0,)), ((), ())), precision=precision, preferred_element_type=F32)


def iota(shape, dim):
    return lax.broadcasted_iota(jnp.int32, shape, dim)


def halves(x):
    high = x.astype(BF16)
    return high, (x - high.astype(F32)).astype(BF16)


def thirds(x):
    high = x.astype(BF16)
    rest = x - high.astype(F32)
    mid = rest.astype(BF16)
    return high, mid, (rest - mid.astype(F32)).astype(BF16)


def picked(table, one_hot, dot):
    high, mid, low = thirds(table)
    return (dot(high, one_hot, None) + dot(mid, one_hot, None)) + dot(low, one_hot, None)


def inverse_factor(s):
    tiles = B // 8
    s = list(s)
    sub, lane = iota((8, B), 0), iota((8, B), 1)
    scale = [jnp.zeros((8, B), F32)] * tiles
    for k0 in range(0, B, GROUP):
        v0 = k0 // 8
        live = range(v0, tiles)
        cols = [{v: jnp.broadcast_to(s[v][:, j : j + 1], (8, B)) for v in live} for j in range(k0, k0 + GROUP)]
        inside = (lane >= k0) & (lane < k0 + GROUP)
        s[v0] = jnp.where(inside, (lane == sub + 8 * v0).astype(F32), s[v0])
        for v in range(v0 + 1, tiles):
            s[v] = jnp.where(inside, 0.0, s[v])
        for j in range(GROUP):
            k = (k0 + j) % 8
            col = cols[j]
            pivot = jnp.broadcast_to(col[v0][k : k + 1, :], (8, B))
            scale[v0] = jnp.where(sub == k, pivot, scale[v0])
            over = 1.0 / pivot
            factor = {v: col[v] * over for v in live}
            factor[v0] = jnp.where(sub > k, factor[v0], 0.0)
            for later in range(j + 1, GROUP):
                at = jnp.broadcast_to(cols[later][v0][k : k + 1, :], (8, B))
                for v in live:
                    cols[later][v] = cols[later][v] - factor[v] * at
            row = jnp.broadcast_to(s[v0][k : k + 1, :], (8, B))
            for v in live:
                s[v] = s[v] - factor[v] * row
    out = []
    for v in range(tiles):
        root = lax.rsqrt(scale[v])
        root = root * (1.5 - 0.5 * scale[v] * root * root)
        out.append(jnp.where(lane <= sub + 8 * v, s[v] * root, 0.0))
    return out


def first_kernel(theta, table, up, left, own, fine, coarse, m_ref, z_ref, g_ref, part_ref, k_ref, d_ref, u_ref, f_ref, y_ref):
    tile_hot = (iota((B, COARSE), 0) == coarse[...] // CP).astype(BF16)
    rows = picked(table[...], tile_hot, tn)
    slot = coarse[...] % CP
    wanted = (iota((4 * CP, COARSE), 0) % CP) == slot
    rows = jnp.where(wanted, rows, 0.0)
    coarse_rows = [jnp.sum(rows[k * CP : (k + 1) * CP], axis=0, keepdims=True) for k in range(4)]
    up_hot = (iota((B, HALF), 0) == fine[:, :HALF]).astype(BF16)
    left_hot = (iota((B, HALF), 0) == fine[:, HALF:]).astype(BF16)
    up_rows = picked(up[...], up_hot, nn)
    left_rows = picked(left[...], left_hot, nn)
    upper_live = (lax.axis_index("row") > 0).astype(F32)
    lane = iota((1, N), 1)
    live = jnp.where((lane >= COARSE) & (lane < COARSE + HALF), upper_live, 1.0)
    across = []
    for k in range(4):
        line = jnp.concatenate(
            [coarse_rows[k], up_rows[k : k + 1] * upper_live, left_rows[k : k + 1], own[k : k + 1, :]], axis=1
        )
        across.append(line / (jnp.exp(jnp.full((1, N), theta[1 + k], F32)) * RANGE_BASE))
    down = jnp.concatenate(across + [live] + [jnp.zeros((B - 5, N), F32)], axis=0).T
    variance = jnp.exp(jnp.full((1, N), theta[0], F32))
    nugget = NUGGET * jnp.exp(jnp.full((1, N), theta[5], F32))
    for r in range(N // B):
        here = slice(r * B, (r + 1) * B)
        squares = []
        for k in range(4):
            gap = down[here, k : k + 1] - across[k]
            squares.append(gap * gap)
        root = ROOT_FIVE * jnp.sqrt((squares[0] + squares[1]) + (squares[2] + squares[3]))
        decay = jnp.exp(-root)
        paired = (down[here, 4:5] * live) * (variance * decay)
        kernel = paired * (1.0 + root + root * root * (1.0 / 3.0))
        common = paired * ((5.0 / 3.0) * (1.0 + root))
        f_ref[0, here, :] = kernel
        for k in range(4):
            f_ref[1 + k, here, :] = common * squares[k]
        same = iota((B, N), 0) + r * B == iota((B, N), 1)
        k_ref[here, :] = kernel + jnp.where(same, live * nugget + 1.0 - live, 0.0)

    def sweep(p, carry):
        at = pl.multiple_of(p * B, B)
        tiles = inverse_factor([k_ref[pl.ds(at + 8 * v, 8), pl.ds(at, B)] for v in range(B // 8)])
        for v in range(B // 8):
            d_ref[8 * v : 8 * (v + 1), :] = tiles[v]

        @pl.when(p < N // B - 1)
        def _():
            d = d_ref[...]
            u_ref[...] = nn(d, k_ref[pl.ds(at, B), :])
            u_ref[:, pl.ds(at, B)] = -d
            k_ref[pl.ds(at, B), :] = jnp.zeros((B, N), F32)
            k_ref[:, pl.ds(at, B)] = jnp.zeros((N, B), F32)
            k_ref[...] -= tn(u_ref[...], u_ref[...])

        return carry

    lax.fori_loop(0, N // B, sweep, 0)
    d = d_ref[...]
    m_ref[:, :LEAD] = -nt(d, k_ref[:LEAD, LEAD:])
    m_ref[:, LEAD:] = d
    m = m_ref[...]
    for i in range(5):
        y_ref[i * B : (i + 1) * B, :] = nn(m, f_ref[i])
    y_ref[5 * B :, :] = m * (live * nugget)
    z_ref[...] = -nn(y_ref[:, :LEAD], k_ref[:LEAD, :LEAD])
    g_ref[...] = nt(y_ref[...], m)

    def folded(x):
        x = jnp.sum(x.reshape(B // 8, 8, x.shape[1]), axis=0)
        total = x[:, :B]
        for c in range(1, x.shape[1] // B):
            total = total + x[:, c * B : (c + 1) * B]
        return total

    sums = []
    for i in range(6):
        for j in range(i + 1):
            lead_part = z_ref[i * B : (i + 1) * B, :] * y_ref[j * B : (j + 1) * B, :LEAD]
            own_part = g_ref[i * B : (i + 1) * B, :] * g_ref[j * B : (j + 1) * B, :]
            sums.append(jnp.sum(2.0 * folded(lead_part) + folded(own_part), axis=0, keepdims=True))
    for i in range(6):
        sums.append(jnp.sum(folded(y_ref[i * B : (i + 1) * B, :] * m), axis=0, keepdims=True))
    sums.append(jnp.zeros((5, B), F32))
    part_ref[...] = jnp.concatenate(sums, axis=0)


def second_kernel(every, up, left, own, fine, coarse, m, z, g, part, white_ref, row_ref, v_ref):
    reps = own.shape[0]
    down = jnp.concatenate([coarse[...], fine[...], jnp.zeros((1, B), jnp.int32)], axis=1)
    down = jnp.broadcast_to(down.astype(F32), (B, N)).T.astype(jnp.int32)[:, :1]
    hot = (down[:COARSE] == iota((COARSE, every.shape[0]), 1)).astype(BF16)
    high, low = halves(every[...])
    v_ref[:COARSE, :] = nn(hot, high, None) + nn(hot, low, None)
    hot = (down[COARSE:LEAD] == iota((B, B), 1)).astype(BF16)
    v_ref[COARSE : COARSE + HALF, :] = picked2(hot[:HALF], up[...])
    v_ref[COARSE + HALF : LEAD, :] = picked2(hot[HALF:], left[...])
    v_ref[LEAD:, :] = own[...].T
    white = nn(m[...], v_ref[...])
    white_ref[...] = white.T
    cross = nt(white, v_ref[:LEAD, :])
    square = nt(white, white)
    lines = []
    eye = (iota((B, B), 0) == iota((B, B), 1)).astype(F32)
    for i in range(6):
        gi = g[i * B : (i + 1) * B, :]
        both = z[i * B : (i + 1) * B, :] * cross
        both = (both[:, :B] + both[:, B : 2 * B]) + (both[:, 2 * B : 3 * B] + both[:, 3 * B :])
        lines.append(jnp.sum(both + 0.5 * (gi * square), axis=0, keepdims=True) - (0.5 * reps) * part[21 + i : 22 + i, :])
    del eye
    whole = jnp.concatenate([(0.5 * reps) * part[:21, :]] + lines + [jnp.zeros((B - 27, B), F32)], axis=0)
    row_ref[...] = jnp.sum(whole.T, axis=0, keepdims=True)


def picked2(one_hot, table):
    high, low = halves(table)
    return nt(one_hot, high, None) + nt(one_hot, low, None)


def third_kernel(rows, step_ref):
    total = jnp.broadcast_to(jnp.sum(rows[...], axis=0, keepdims=True), (8, B))
    sub, lane = iota((8, B), 0), iota((8, B), 1)
    a = jnp.zeros((8, B), F32)
    for i in range(6):
        for j in range(6):
            low, high = min(i, j), max(i, j)
            entry = jnp.broadcast_to(total[:, high * (high + 1) // 2 + low : high * (high + 1) // 2 + low + 1], (8, B))
            a = jnp.where((sub == i) & (lane == j), entry, a)
        entry = jnp.broadcast_to(total[:, 21 + i : 22 + i], (8, B))
        a = jnp.where((sub == i) & (lane == 6), entry, a)
    for k in range(6):
        row = jnp.broadcast_to(a[k : k + 1, :], (8, B))
        col = jnp.broadcast_to(a[:, k : k + 1], (8, B))
        row = row / jnp.broadcast_to(row[:, k : k + 1], (8, B))
        a = jnp.where(sub == k, row, a - col * row)
    step_ref[...] = a


def body(coords, values, coarse_coords, coarse_values, fine_index, coarse_index, log_params):
    reps = values.shape[0]
    devices = lax.axis_size("row") * lax.axis_size("col")
    every = lax.all_gather(coarse_values.T, AXES, axis=0, tiled=True)
    up_coords = shifted(coords, "row", 1)
    left_coords = passed_along(coords, "col", 1)
    up_values = shifted(values, "row", 1)
    left_values = passed_along(values, "col", 1)
    table = lax.all_to_all(
        jnp.broadcast_to(coarse_coords.reshape(1, 4 * CP), (devices, 4 * CP)), AXES, 0, 0, tiled=True
    )
    vmem = pl.BlockSpec(memory_space=pltpu.VMEM)
    smem = pl.BlockSpec(memory_space=pltpu.SMEM)
    m, z, g, part = pl.pallas_call(
        first_kernel,
        out_shape=(
            jax.ShapeDtypeStruct((B, N), F32),
            jax.ShapeDtypeStruct((6 * B, LEAD), F32),
            jax.ShapeDtypeStruct((6 * B, B), F32),
            jax.ShapeDtypeStruct((32, B), F32),
        ),
        in_specs=[smem] + [vmem] * 6,
        out_specs=(vmem,) * 4,
        scratch_shapes=[
            pltpu.VMEM((N, N), F32),
            pltpu.VMEM((B, B), F32),
            pltpu.VMEM((B, N), F32),
            pltpu.VMEM((5, N, N), F32),
            pltpu.VMEM((6 * B, N), F32),
        ],
        compiler_params=pltpu.CompilerParams(vmem_limit_bytes=40 * 2**20),
        name="fisher_part",
    )(log_params, table, up_coords, left_coords, coords, fine_index, coarse_index)
    white, row = pl.pallas_call(
        second_kernel,
        out_shape=(jax.ShapeDtypeStruct((reps, B), F32), jax.ShapeDtypeStruct((1, B), F32)),
        in_specs=[vmem] * 10,
        out_specs=(vmem,) * 2,
        scratch_shapes=[pltpu.VMEM((N, reps), F32)],
        compiler_params=pltpu.CompilerParams(vmem_limit_bytes=40 * 2**20),
        name="gradient_part",
    )(every, up_values, left_values, values, fine_index, coarse_index, m, z, g, part)
    rows = lax.all_to_all(jnp.broadcast_to(row, (devices, B)), AXES, 0, 0, tiled=True)
    step = pl.pallas_call(
        third_kernel,
        out_shape=jax.ShapeDtypeStruct((8, B), F32),
        in_specs=[vmem],
        out_specs=vmem,
        name="solve_part",
    )(rows)
    return (step[:6, 6], white)


def solution(mesh):
    in_specs = (
        P(None, AXES),
        P(None, AXES),
        P(None, AXES),
        P(None, AXES),
        P(AXES, None),
        P(AXES, None),
        P(),
    )
    out_specs = (P(), P(None, AXES))
    return jax.shard_map(body, mesh=mesh, in_specs=in_specs, out_specs=out_specs, check_vma=False)
```

time: 630 us -> 117 us (0.19); the launches traced: 622 us -> 117 us
  other arithmetic: 197 us -> 0 us
  matrix products: 183 us -> 0 us
  blocking collectives: 123 us -> 15.2 us
  local copies, waits for them, and re-layouts: 88.8 us -> 9.98 us
  Pallas kernels: 0 us -> 48.2 us
  starting transfers between devices: 9.66 us -> 20.2 us
  waiting for transfers between devices: 0.05 us -> 9.24 us
    another operation x26 -> x0, other arithmetic: 182 us -> none  [the longest x18 126 us: fisher_terms(): factor = jnp.linalg.cholesky(cov)]
    dot_general x11 -> x0, matrix products: 157 us -> none  [the longest x1 34.7 us: fisher_terms(): jnp.einsum('iab,jba->ij', joint_prod, joint_prod, precision=HIGH)]
    psum x1 -> x0, blocking collectives: 64.6 us -> none  [body(): grad, fisher = lax.psum((grad, fisher), ('row', 'col'))]
    all_gather x1 -> x0, blocking collectives: 58.2 us -> none  [body(): lax.all_gather(coarse_coords, ('row', 'col'), axis=1, tiled=True)]
    pallas_call x0 -> x3, Pallas kernels: none -> 48.2 us  [the longest x1 40.9 us: body(): pl.pallas_call(first_kernel, out_shape=(jax.ShapeDtypeStruct((B, N), F32)...]
    another operation x19 -> x0, matrix products: 26.4 us -> none  [the longest x8 14.2 us: fisher_terms(): factor = jnp.linalg.cholesky(cov)]
    another operation x21 -> x0, local copies, waits for them, and re-layouts: 26.2 us -> none
    transpose x2 -> x0, local copies, waits for them, and re-layouts: 24.1 us -> none  [the longest x1 14.3 us: fisher_terms(): joint_prod = jnp.einsum('ab,ibc->iac', joint_prec, derivs, precision=HIGH)]
  transfers between devices with their start and end apart: 5 -> 6, of which waited for: 0 -> 2; matrix products, arithmetic and copies ran while one was open for 64% -> 1% of each run, Pallas kernels for 0% -> 35%
where the time goes in v1:
time: 117 us
  Pallas kernels  48.2 us (41%)
  starting transfers between devices  20.2 us (17%)
  blocking collectives  15.2 us (13%)
  between operations  14.1 us (12%)
  local copies, waits for them, and re-layouts  9.98 us (9%)
  waiting for transfers between devices  9.24 us (8%)
    pallas_call x1, Pallas kernels, body(): pl.pallas_call(first_kernel, out_shape=(jax.ShapeDtypeStruct((B, N), F32)...  40.9 us
    all_to_all x1, blocking collectives, body(): lax.all_to_all(jnp.broadcast_to(row, (devices, B)), AXES, 0, 0, tiled=True)  15.2 us
    all_to_all x1, starting transfers between devices, body(): lax.all_to_all(jnp.broadcast_to(coarse_coords.reshape(1, 4 * CP), (device...  9.52 us
    ppermute x2, starting transfers between devices, shifted(): lax.ppermute(value, axis, [(source, source + steps) for source in range(f...  8.05 us
    unnamed x16, local copies, waits for them, and re-layouts  7.14 us
    ppermute x2, waiting for transfers between devices, passed_along(): return lax.ppermute(block, axis, route)  5.38 us
    pallas_call x1, Pallas kernels, body(): pl.pallas_call(second_kernel, out_shape=(jax.ShapeDtypeStruct((reps, B),...  5.03 us
    all_gather x1, waiting for transfers between devices, body(): every = lax.all_gather(coarse_values.T, AXES, axis=0, tiled=True)  3.17 us
  transfers between devices with their start and end apart: 6, of which 2 were waited for; matrix products, arithmetic and copies ran while one was open for 1% of the time, Pallas kernels for 35%

profile of v1, /device:TPU:1, one launch (start us, length us, event | category | flops | bytes accessed | tf_op | source)
XLA Modules:
  0.0 116.9 jit_solution(833508024957352675)
XLA Ops:
  7.2 0.0 all-gather.2.cloned.1.call-start
  7.2 0.7 all-gather.2.cloned.1.call-update
  7.9 4.5 %collective-permute-start = (f32[512,128]{1,0:T(8,128)}, f32[512,128]{1,0:T(8,128)S(1)}, u32[]{:S(2)}, u32[]{:S(2)}) collective-permute-start(f32[512,128]{1,0:T(8,128)} %own.3), channel_id=1, source_target_pairs={{0,16},{16,32},{32,48},{48,64},{64,80},{80,96},{96,112},{1,17},{17... | collective-permute-start | bytes 786440 | tf_op jit(solution)/shard_map/ppermute | solution.py:30
  12.4 1.4 %collective-permute-start.1 = (f32[512,128]{1,0:T(8,128)}, f32[512,128]{1,0:T(8,128)S(1)}, u32[]{:S(2)}, u32[]{:S(2)}) collective-permute-start(f32[512,128]{1,0:T(8,128)} %own.3), channel_id=1, source_target_pairs={{15,0},{0,1},{1,2},{2,3},{3,4},{4,5},{5,6},{6,7},{7,8},{8,9},{9,10... | collective-permute-start | bytes 786440 | tf_op jit(solution)/shard_map/ppermute | solution.py:36
  13.8 0.8 broadcast_in_dim.12
  14.5 0.7 broadcast_in_dim.13
  15.2 9.5 %all-to-all-start = ((f32[128,1,64]{2,1,0:T(1,128)}), f32[128,1,64]{2,1,0:T(1,128)S(1)}, u32[]{:S(2)}, u32[]{:S(2)}) async-start(f32[128,1,64]{2,1,0:T(1,128)} %broadcast_in_dim.13), calls=%async_computation | async-start | bytes 131072 | tf_op jit(solution)/shard_map/all_to_all | solution.py:254
  24.7 3.5 %collective-permute-start.2 = (f32[4,128]{1,0:T(4,128)}, f32[4,128]{1,0:T(4,128)S(1)}, u32[]{:S(2)}, u32[]{:S(2)}) collective-permute-start(f32[4,128]{1,0:T(4,128)} %own.2), channel_id=1, source_target_pairs={{0,16},{16,32},{32,48},{48,64},{64,80},{80,96},{96,112},{1,17},{17... | collective-permute-start | bytes 6152 | tf_op jit(solution)/shard_map/ppermute | solution.py:30
  28.3 1.3 %collective-permute-start.3 = (f32[4,128]{1,0:T(4,128)}, f32[4,128]{1,0:T(4,128)S(1)}, u32[]{:S(2)}, u32[]{:S(2)}) collective-permute-start(f32[4,128]{1,0:T(4,128)} %own.2), channel_id=1, source_target_pairs={{15,0},{0,1},{1,2},{2,3},{3,4},{4,5},{5,6},{6,7},{7,8},{8,9},{9,10... | collective-permute-start | bytes 6152 | tf_op jit(solution)/shard_map/ppermute | solution.py:36
  29.5 5.4 %collective-permute-done.3.left = f32[4,128]{1,0:T(4,128)S(1)} collective-permute-done((f32[4,128]{1,0:T(4,128)}, f32[4,128]{1,0:T(4,128)S(1)}, u32[]{:S(2)}, u32[]{:S(2)}) %collective-permute-start.3) | collective-permute-done | bytes 2080 | tf_op jit(solution)/shard_map/ppermute | solution.py:36
  34.9 0.7 copy-done.2
  35.6 0.7 copy-done.4
  36.3 0.7 copy-done.6
  37.0 0.7 copy-done.7
  37.6 40.9 %fisher_part.1 = (f32[128,640]{1,0:T(8,128)S(1)}, f32[768,512]{1,0:T(8,128)S(1)}, f32[768,128]{1,0:T(8,128)S(1)}, f32[32,128]{1,0:T(8,128)S(1)}) custom-call(f32[6]{0:T(128)S(1)} %copy-done.7, f32[128,64]{1,0:T(8,128)S(1)} %bitcast.4, f32[4,128]{1,0:T(4,128)S(1)} %collective-permute-done.2.up, f32[4,128]{1,0:T(4,128)S(1)} %collective-permute-done.3.left, ...), custom_call_target="tpu_custom_call" | custom-call | tf_op jit(solution)/shard_map/fisher_part/pallas_call | solution.py:259
  78.6 3.2 %all-gather.2.cloned.1.call-done.every = f32[2048,512]{1,0:T(8,128)} async-done(((f32[16,512]{1,0:T(8,128)}), f32[2048,512]{1,0:T(8,128)}) %all-gather.2.cloned.1.call-update) | async-done | bytes 4194320 | tf_op jit(solution)/shard_map/all_gather | solution.py:249
  81.8 2.2 %copy-done = f32[2048,512]{1,0:T(8,128)S(1)} copy-done((f32[2048,512]{1,0:T(8,128)S(1)}, f32[2048,512]{1,0:T(8,128)}, u32[]{:S(2)}) %copy-start) | copy-done | bytes 4194328
  83.9 0.9 copy-done.1
  84.9 0.7 copy-done.3
  85.6 0.7 copy-done.5
  86.2 5.0 %gradient_part.1 = (f32[512,128]{1,0:T(8,128)}, f32[1,128]{1,0:T(1,128)S(1)}) custom-call(f32[2048,512]{1,0:T(8,128)S(1)} %copy-done, f32[512,128]{1,0:T(8,128)S(1)} %collective-permute-done.up, f32[512,128]{1,0:T(8,128)S(1)} %collective-permute-done.1.left, f32[512,128]{1,0:T(8,128)S(1)} %copy-done.1, s32[1,128]{1,0:T(1,128)S(1)} %copy-done.5, ...), custom_call_target="tpu_custom_call" | custom-call | tf_op jit(solution)/shard_map/gradient_part/pallas_call | solution.py:279
  91.3 15.2 %all_to_all.16 = f32[128,1,128]{2,1,0:T(1,128)} all-to-all(f32[128,1,128]{2,1,0:T(1,128)S(1)} %broadcast_in_dim.14), channel_id=1, replica_groups=mesh['row'=8,'col'=16] {'row','col'}, dimensions={0} | all-to-all | bytes 131072 | tf_op jit(solution)/shard_map/all_to_all | solution.py:288
  106.5 2.2 %solve_part.1 = f32[8,128]{1,0:T(8,128)} custom-call(f32[128,128]{1,0:T(8,128)} %bitcast.6), custom_call_target="tpu_custom_call" | custom-call | tf_op jit(solution)/shard_map/solve_part/pallas_call | solution.py:289
  108.7 1.4 %slice_reduce_fusion = f32[6]{0:T(128)} fusion(f32[8,128]{1,0:T(8,128)} %solve_part.1), kind=kLoop, calls=%fused_computation | loop fusion | bytes 48 | tf_op jit(solution)/shard_map/slice | solution.py:296
  (13 shorter events, 0.1 us)
Async XLA Ops:
  7.2 74.6 %all-gather.2.cloned.1.call-start = ((), (), s32[]{:S(2)}) async-start(), calls=%async_computation.2 | async-start | bytes 4227072 | tf_op jit(solution)/shard_map/all_gather | solution.py:249
  7.9 70.7 %collective-permute-start = (f32[512,128]{1,0:T(8,128)}, f32[512,128]{1,0:T(8,128)S(1)}, u32[]{:S(2)}, u32[]{:S(2)}) collective-permute-start(f32[512,128]{1,0:T(8,128)} %own.3), channel_id=1, source_target_pairs={{0,16},{16,32},{32,48},{48,64},{64,80},{80,96},{96,112},{1,17},{17... | collective-permute-start | bytes 786440 | tf_op jit(solution)/shard_map/ppermute | solution.py:30
  12.4 66.2 %collective-permute-start.1 = (f32[512,128]{1,0:T(8,128)}, f32[512,128]{1,0:T(8,128)S(1)}, u32[]{:S(2)}, u32[]{:S(2)}) collective-permute-start(f32[512,128]{1,0:T(8,128)} %own.3), channel_id=1, source_target_pairs={{15,0},{0,1},{1,2},{2,3},{3,4},{4,5},{5,6},{6,7},{7,8},{8,9},{9,10... | collective-permute-start | bytes 786440 | tf_op jit(solution)/shard_map/ppermute | solution.py:36
  15.2 19.7 %all-to-all-start = ((f32[128,1,64]{2,1,0:T(1,128)}), f32[128,1,64]{2,1,0:T(1,128)S(1)}, u32[]{:S(2)}, u32[]{:S(2)}) async-start(f32[128,1,64]{2,1,0:T(1,128)} %broadcast_in_dim.13), calls=%async_computation | async-start | bytes 131072 | tf_op jit(solution)/shard_map/all_to_all | solution.py:254
  24.7 4.8 %collective-permute-start.2 = (f32[4,128]{1,0:T(4,128)}, f32[4,128]{1,0:T(4,128)S(1)}, u32[]{:S(2)}, u32[]{:S(2)}) collective-permute-start(f32[4,128]{1,0:T(4,128)} %own.2), channel_id=1, source_target_pairs={{0,16},{16,32},{32,48},{48,64},{64,80},{80,96},{96,112},{1,17},{17... | collective-permute-start | bytes 6152 | tf_op jit(solution)/shard_map/ppermute | solution.py:30
  28.3 6.6 %collective-permute-start.3 = (f32[4,128]{1,0:T(4,128)}, f32[4,128]{1,0:T(4,128)S(1)}, u32[]{:S(2)}, u32[]{:S(2)}) collective-permute-start(f32[4,128]{1,0:T(4,128)} %own.2), channel_id=1, source_target_pairs={{15,0},{0,1},{1,2},{2,3},{3,4},{4,5},{5,6},{6,7},{7,8},{8,9},{9,10... | collective-permute-start | bytes 6152 | tf_op jit(solution)/shard_map/ppermute | solution.py:36
  34.9 0.7 copy-start.2
  35.6 0.7 copy-start.4
  36.3 0.7 copy-start.6
  37.0 0.7 copy-start.7
  81.7 2.2 %copy-start = (f32[2048,512]{1,0:T(8,128)S(1)}, f32[2048,512]{1,0:T(8,128)}, u32[]{:S(2)}) copy-start(f32[2048,512]{1,0:T(8,128)} %all-gather.2.cloned.1.call-done.every) | copy-start | bytes 12582916
  83.9 0.9 copy-start.1
  84.9 0.7 copy-start.3
  85.6 0.7 copy-start.5
Sparse Core Ops, SparseCore 0:
  11.1 70.5 all-gather.1

commit v2 on v1

v2 whole, which is shorter than its diff:
```python
import math

import jax
import jax.numpy as jnp
from jax import lax
from jax.experimental import pallas as pl
from jax.experimental.pallas import tpu as pltpu
from jax.sharding import PartitionSpec as P

HIGH = lax.Precision.HIGHEST
ROOT_FIVE = math.sqrt(5.0)
NUGGET = 0.2
RANGE_BASE = 0.5
F32 = jnp.float32
BF16 = jnp.bfloat16
AXES = ("row", "col")

B = 128
N = 640
LEAD = 512
COARSE = 384
HALF = 64
CP = 16
MOST = 6
GROUP = 8


def shifted(value, axis, steps):
    count = lax.axis_size(axis)
    first, last = (max(0, -steps), min(count, count - steps))
    return lax.ppermute(value, axis, [(source, source + steps) for source in range(first, last)])


def passed_along(block, axis, distance):
    devices = range(lax.axis_size(axis))
    route = [((i - distance) % len(devices), i) for i in devices]
    return lax.ppermute(block, axis, route)


def nn(a, b, precision=HIGH):
    return lax.dot_general(a, b, (((1,), (0,)), ((), ())), precision=precision, preferred_element_type=F32)


def nt(a, b, precision=HIGH):
    return lax.dot_general(a, b, (((1,), (1,)), ((), ())), precision=precision, preferred_element_type=F32)


def tn(a, b, precision=HIGH):
    return lax.dot_general(a, b, (((0,), (0,)), ((), ())), precision=precision, preferred_element_type=F32)


def iota(shape, dim):
    return lax.broadcasted_iota(jnp.int32, shape, dim)


def halves(x):
    high = x.astype(BF16)
    return high, (x - high.astype(F32)).astype(BF16)


def thirds(x):
    high = x.astype(BF16)
    rest = x - high.astype(F32)
    mid = rest.astype(BF16)
    return high, mid, (rest - mid.astype(F32)).astype(BF16)


def picked(table, one_hot, dot):
    high, mid, low = thirds(table)
    return (dot(high, one_hot, None) + dot(mid, one_hot, None)) + dot(low, one_hot, None)


def six_left(x):
    one, two, three = thirds(x)
    return jnp.concatenate([one, one, two, two, one, three], axis=1)


def six_right(x):
    one, two, three = thirds(x)
    return jnp.concatenate([one, two, one, two, three, one], axis=0)


def three_terms(left, right, dot):
    rows = left[0].shape[0]
    both = dot(jnp.concatenate(left, axis=0), right[0], None)
    return (both[:rows] + both[rows:]) + dot(left[0], right[1], None)


def inverse_factor(s):
    tiles = B // 8
    s = list(s)
    sub, lane = iota((8, B), 0), iota((8, B), 1)
    scale = [jnp.zeros((8, B), F32)] * tiles
    for k0 in range(0, B, GROUP):
        v0 = k0 // 8
        live = range(v0, tiles)
        cols = [{v: jnp.broadcast_to(s[v][:, j : j + 1], (8, B)) for v in live} for j in range(k0, k0 + GROUP)]
        inside = (lane >= k0) & (lane < k0 + GROUP)
        s[v0] = jnp.where(inside, (lane == sub + 8 * v0).astype(F32), s[v0])
        for v in range(v0 + 1, tiles):
            s[v] = jnp.where(inside, 0.0, s[v])
        for j in range(GROUP):
            k = (k0 + j) % 8
            col = cols[j]
            pivot = jnp.broadcast_to(col[v0][k : k + 1, :], (8, B))
            scale[v0] = jnp.where(sub == k, pivot, scale[v0])
            over = 1.0 / pivot
            factor = {v: col[v] * over for v in live}
            factor[v0] = jnp.where(sub > k, factor[v0], 0.0)
            for later in range(j + 1, GROUP):
                at = jnp.broadcast_to(cols[later][v0][k : k + 1, :], (8, B))
                for v in live:
                    cols[later][v] = cols[later][v] - factor[v] * at
            row = jnp.broadcast_to(s[v0][k : k + 1, :], (8, B))
            for v in live:
                s[v] = s[v] - factor[v] * row
    out = []
    for v in range(tiles):
        root = lax.rsqrt(scale[v])
        root = root * (1.5 - 0.5 * scale[v] * root * root)
        out.append(jnp.where(lane <= sub + 8 * v, s[v] * root, 0.0))
    return out


def request_kernel(coarse_coords, coarse, coords, values, out_ref, place_ref, tile_ref):
    reps = values.shape[0]
    tile_ref[:reps, :] = values[...]
    tile_ref[reps:, :] = jnp.concatenate([coords[...], jnp.zeros((4, B), F32)], axis=0)
    tile, slot = coarse[...] // CP, coarse[...] % CP
    hot = (iota((B, COARSE), 0) == tile).astype(BF16)
    earlier = (iota((COARSE, COARSE), 0) < iota((COARSE, COARSE), 1)).astype(BF16)
    rank = jnp.sum(hot.astype(F32) * nn(hot, earlier, None), axis=0, keepdims=True).astype(jnp.int32)
    place_ref[...] = tile * MOST + rank
    asked = jnp.where(iota((B, COARSE), 0) == rank + 4 * CP, slot, 0).astype(F32).astype(BF16)
    line = jnp.concatenate([coarse_coords[k : k + 1, :] for k in range(4)] + [jnp.zeros((1, B - 4 * CP), F32)], axis=1)
    out_ref[...] = line + nt(hot, asked, None)


def send_kernel(table, coarse_values, after, send_ref):
    del after
    three = jnp.concatenate(thirds(coarse_values[...]), axis=0)
    slots = (iota((B, 3 * CP), 1) % CP).astype(F32)
    chunks = coarse_values.shape[1] // B
    for r in range(MOST):
        hot = (table[:, 4 * CP + r : 4 * CP + r + 1] == slots).astype(BF16)
        rows = nn(hot, three, None)
        for c in range(chunks):
            send_ref[pl.ds(r * chunks + c, B, stride=MOST * chunks), :] = rows[:, c * B : (c + 1) * B]


def spreads(theta, k, count):
    return jnp.exp(jnp.full((1, count), theta[1 + k], F32)) * RANGE_BASE


def pair(down, across, theta, live_down, live_across):
    squares = []
    for k in range(4):
        gap = down[:, k : k + 1] - across[k]
        squares.append(gap * gap)
    root = ROOT_FIVE * jnp.sqrt((squares[0] + squares[1]) + (squares[2] + squares[3]))
    variance = jnp.exp(jnp.full((1, live_across.shape[1]), theta[0], F32))
    paired = (live_down * live_across) * (variance * jnp.exp(-root))
    return paired * (1.0 + root + root * root * (1.0 / 3.0)), paired * ((5.0 / 3.0) * (1.0 + root)), squares


def nugget_of(theta, count):
    return NUGGET * jnp.exp(jnp.full((1, count), theta[5], F32))


def fine_kernel(theta, up, left, own, fine, d_ref, line_ref):
    up_hot = (iota((B, HALF), 0) == fine[:, :HALF]).astype(BF16)
    left_hot = (iota((B, HALF), 0) == fine[:, HALF:]).astype(BF16)
    upper_live = (lax.axis_index("row") > 0).astype(F32)
    picks = jnp.concatenate([picked(up[-8:, :], up_hot, nn) * upper_live, picked(left[-8:, :], left_hot, nn)], axis=1)
    across = [picks[k : k + 1] / spreads(theta, k, B) for k in range(4)]
    live = jnp.where(iota((1, B), 1) < HALF, upper_live, 1.0)
    lines = jnp.concatenate(across + [live, jnp.zeros((3, B), F32)], axis=0)
    line_ref[:, :B] = lines
    own_lines = [own[k : k + 1, :] / spreads(theta, k, B) for k in range(4)]
    line_ref[:, B:] = jnp.concatenate(own_lines + [jnp.ones((1, B), F32), jnp.zeros((3, B), F32)], axis=0)
    down = jnp.concatenate([lines, jnp.zeros((B - 8, B), F32)], axis=0).T
    kernel, _, _ = pair(down, across, theta, down[:, 4:5], live)
    same = iota((B, B), 0) == iota((B, B), 1)
    cov = kernel + jnp.where(same, live * nugget_of(theta, B) + 1.0 - live, 0.0)
    tiles = inverse_factor([cov[8 * v : 8 * (v + 1)] for v in range(B // 8)])
    for v in range(B // 8):
        d_ref[8 * v : 8 * (v + 1), :] = tiles[v]


def first_kernel(theta, table, lines, d_fine, coarse, m_ref, z_ref, g_ref, part_ref, k_ref, s_ref, d_ref, u_ref, left_ref, right_ref, f1_ref, f2_ref, f3_ref, y_ref):
    tile_hot = (iota((B, COARSE), 0) == coarse[...] // CP).astype(BF16)
    rows = picked(table[:, : 4 * CP], tile_hot, tn)
    wanted = (iota((4 * CP, COARSE), 0) % CP) == coarse[...] % CP
    rows = jnp.where(wanted, rows, 0.0)
    across = []
    for k in range(4):
        line = jnp.sum(rows[k * CP : (k + 1) * CP], axis=0, keepdims=True) / spreads(theta, k, COARSE)
        across.append(jnp.concatenate([lines[k : k + 1, :B], line, lines[k : k + 1, B:]], axis=1))
    live = jnp.concatenate([lines[4:5, :B], jnp.ones((1, N - B), F32)], axis=1)
    down = jnp.concatenate(across + [live] + [jnp.zeros((B - 5, N), F32)], axis=0).T
    nugget = nugget_of(theta, N)
    for r in range(N // B):
        here = slice(r * B, (r + 1) * B)
        kernel, common, squares = pair(down[here], across, theta, down[here, 4:5], live)
        for i, part in enumerate([kernel] + [common * square for square in squares]):
            f1_ref[i, here, :], f2_ref[i, here, :], f3_ref[i, here, :] = thirds(part)
        same = iota((B, N), 0) + r * B == iota((B, N), 1)
        k_ref[here, :] = kernel + jnp.where(same, live * nugget + 1.0 - live, 0.0)

    def prepare(p, d):
        at = pl.multiple_of(p * B, B)
        after = pl.multiple_of(p * B + B, B)
        u_ref[...] = nn(six_left(d), six_right(k_ref[pl.ds(at, B), :]), None)
        u_ref[:, pl.ds(at, B)] = -d
        k_ref[pl.ds(at, B), :] = jnp.zeros((B, N), F32)
        k_ref[:, pl.ds(at, B)] = jnp.zeros((N, B), F32)
        left_ref[...] = six_left(u_ref[...].T)
        right_ref[...] = six_right(u_ref[...])
        s_ref[...] = k_ref[pl.ds(after, B), pl.ds(after, B)] - nn(
            left_ref[pl.ds(after, B), :], right_ref[:, pl.ds(after, B)], None
        )

    prepare(0, d_fine[...])

    def sweep(p, carry):
        tiles = inverse_factor([s_ref[8 * v : 8 * (v + 1), :] for v in range(B // 8)])
        k_ref[...] -= nn(left_ref[...], right_ref[...], None)
        for v in range(B // 8):
            d_ref[8 * v : 8 * (v + 1), :] = tiles[v]

        @pl.when(p < N // B - 1)
        def _():
            prepare(p, d_ref[...])

        return carry

    lax.fori_loop(1, N // B, sweep, 0)
    d = d_ref[...]
    m_ref[:, :LEAD] = -nt(d, k_ref[:LEAD, LEAD:])
    m_ref[:, LEAD:] = d
    m = m_ref[...]
    parts = thirds(m)
    for i in range(5):
        first = nn(jnp.concatenate(parts, axis=0), f1_ref[i], None)
        second = nn(jnp.concatenate(parts[:2], axis=0), f2_ref[i], None)
        small = (first[2 * B :] + second[B:]) + nn(parts[0], f3_ref[i], None)
        y_ref[i * B : (i + 1) * B, :] = first[:B] + ((first[B : 2 * B] + second[:B]) + small)
    y_ref[5 * B :, :] = m * (live * nugget)
    high, low = halves(y_ref[...])
    z_ref[...] = -three_terms((high[:, :LEAD], low[:, :LEAD]), halves(k_ref[:LEAD, :LEAD]), nn)
    g_ref[...] = three_terms((high, low), parts[:2], nt)

    def folded(x):
        x = jnp.sum(x.reshape(B // 8, 8, x.shape[1]), axis=0)
        total = x[:, :B]
        for c in range(1, x.shape[1] // B):
            total = total + x[:, c * B : (c + 1) * B]
        return total

    sums = []
    for i in range(6):
        for j in range(i + 1):
            lead_part = z_ref[i * B : (i + 1) * B, :] * y_ref[j * B : (j + 1) * B, :LEAD]
            own_part = g_ref[i * B : (i + 1) * B, :] * g_ref[j * B : (j + 1) * B, :]
            sums.append(jnp.sum(2.0 * folded(lead_part) + folded(own_part), axis=0, keepdims=True))
    for i in range(6):
        sums.append(jnp.sum(folded(y_ref[i * B : (i + 1) * B, :] * m), axis=0, keepdims=True))
    sums.append(jnp.zeros((5, B), F32))
    part_ref[...] = jnp.concatenate(sums, axis=0)


def picked2(one_hot, table):
    high, low = halves(table)
    return nt(one_hot, high, None) + nt(one_hot, low, None)


def second_kernel(arrived, place, up, left, own, fine, m, z, g, part, white_ref, row_ref, v_ref):
    reps = own.shape[0]
    chunks = reps // B
    held = arrived.shape[0] // chunks
    down = jnp.concatenate([fine[...], place[...], jnp.zeros((1, B), jnp.int32)], axis=1)
    down = jnp.broadcast_to(down.astype(F32), (B, N)).T.astype(jnp.int32)[:, :1]
    hot = (down[:B] == iota((B, B), 1)).astype(BF16)
    v_ref[:HALF, :] = picked2(hot[:HALF], up[:reps, :])
    v_ref[HALF:B, :] = picked2(hot[HALF:], left[:reps, :])
    v_ref[LEAD:, :] = own[...].T
    hot = (down[B:LEAD] == iota((COARSE, held), 1)).astype(BF16)
    for c in range(chunks):
        high, low = halves(arrived[pl.ds(c, held, stride=chunks), :])
        v_ref[B:LEAD, c * B : (c + 1) * B] = nn(hot, high, None) + nn(hot, low, None)
    white = nn(m[...], v_ref[...])
    white_ref[...] = white.T
    cross = nt(white, v_ref[:LEAD, :])
    square = nt(white, white)
    lines = []
    for i in range(6):
        both = z[i * B : (i + 1) * B, :] * cross
        both = (both[:, :B] + both[:, B : 2 * B]) + (both[:, 2 * B : 3 * B] + both[:, 3 * B :])
        both = both + 0.5 * (g[i * B : (i + 1) * B, :] * square)
        lines.append(jnp.sum(both, axis=0, keepdims=True) - (0.5 * reps) * part[21 + i : 22 + i, :])
    whole = jnp.concatenate([(0.5 * reps) * part[:21, :]] + lines + [jnp.zeros((B - 27, B), F32)], axis=0)
    row_ref[...] = jnp.broadcast_to(jnp.sum(whole.T, axis=0, keepdims=True), row_ref.shape)


def third_kernel(rows, step_ref):
    total = jnp.broadcast_to(jnp.sum(rows[...], axis=0, keepdims=True), (8, B))
    sub, lane = iota((8, B), 0), iota((8, B), 1)
    a = jnp.zeros((8, B), F32)
    for i in range(6):
        for j in range(6):
            low, high = min(i, j), max(i, j)
            entry = jnp.broadcast_to(total[:, high * (high + 1) // 2 + low : high * (high + 1) // 2 + low + 1], (8, B))
            a = jnp.where((sub == i) & (lane == j), entry, a)
        entry = jnp.broadcast_to(total[:, 21 + i : 22 + i], (8, B))
        a = jnp.where((sub == i) & (lane == 6), entry, a)
    for k in range(6):
        row = jnp.broadcast_to(a[k : k + 1, :], (8, B))
        col = jnp.broadcast_to(a[:, k : k + 1], (8, B))
        row = row / jnp.broadcast_to(row[:, k : k + 1], (8, B))
        a = jnp.where(sub == k, row, a - col * row)
    step_ref[...] = jnp.sum(jnp.where((lane == sub) & (sub < 6), jnp.broadcast_to(a[:, 6:7], (8, B)), 0.0), axis=0)[:6]


def body(coords, values, coarse_coords, coarse_values, fine_index, coarse_index, log_params):
    reps = values.shape[0]
    devices = lax.axis_size("row") * lax.axis_size("col")
    vmem = pl.BlockSpec(memory_space=pltpu.VMEM)
    smem = pl.BlockSpec(memory_space=pltpu.SMEM)
    large = pltpu.CompilerParams(vmem_limit_bytes=60 * 2**20)

    def shape(*dims):
        return jax.ShapeDtypeStruct(dims, F32)

    def cost(flops):
        return pl.CostEstimate(flops=flops, bytes_accessed=2**20, transcendentals=0)

    request, place, tile = pl.pallas_call(
        request_kernel,
        out_shape=(shape(devices, B), jax.ShapeDtypeStruct((1, COARSE), jnp.int32), shape(reps + 8, B)),
        in_specs=[vmem] * 4,
        out_specs=(vmem,) * 3,
        compiler_params=large,
        name="request_part",
    )(coarse_coords, coarse_index, coords, values)
    up = shifted(tile, "row", 1)
    left = passed_along(tile, "col", 1)
    table = lax.all_to_all(request, AXES, 0, 0, tiled=True)
    d_fine, lines = pl.pallas_call(
        fine_kernel,
        out_shape=(shape(B, B), shape(8, 2 * B)),
        in_specs=[smem] + [vmem] * 4,
        out_specs=(vmem,) * 2,
        compiler_params=large,
        cost_estimate=cost(4 * 10**9),
        name="fine_part",
    )(log_params, up, left, coords, fine_index)
    send = pl.pallas_call(
        send_kernel,
        out_shape=shape(devices * MOST * reps // B, B),
        in_specs=[vmem] * 2 + [pl.BlockSpec(memory_space=pl.ANY)],
        out_specs=vmem,
        compiler_params=large,
        name="send_part",
    )(table, coarse_values.T, lines)
    arrived = lax.all_to_all(send, AXES, 0, 0, tiled=True)
    m, z, g, part = pl.pallas_call(
        first_kernel,
        out_shape=(shape(B, N), shape(6 * B, LEAD), shape(6 * B, B), shape(32, B)),
        in_specs=[smem] + [vmem] * 4,
        out_specs=(vmem,) * 4,
        scratch_shapes=[
            pltpu.VMEM((N, N), F32),
            pltpu.VMEM((B, B), F32),
            pltpu.VMEM((B, B), F32),
            pltpu.VMEM((B, N), F32),
            pltpu.VMEM((N, 6 * B), BF16),
            pltpu.VMEM((6 * B, N), BF16),
            pltpu.VMEM((5, N, N), BF16),
            pltpu.VMEM((5, N, N), BF16),
            pltpu.VMEM((5, N, N), BF16),
            pltpu.VMEM((6 * B, N), F32),
        ],
        compiler_params=large,
        cost_estimate=cost(30 * 10**9),
        name="fisher_part",
    )(log_params, table, lines, d_fine, coarse_index)
    white, row = pl.pallas_call(
        second_kernel,
        out_shape=(shape(reps, B), shape(devices, B)),
        in_specs=[vmem] * 10,
        out_specs=(vmem,) * 2,
        scratch_shapes=[pltpu.VMEM((N, reps), F32)],
        compiler_params=large,
        name="gradient_part",
    )(arrived, place, up, left, values, fine_index, m, z, g, part)
    rows = lax.all_to_all(row, AXES, 0, 0, tiled=True)
    step = pl.pallas_call(
        third_kernel,
        out_shape=shape(6),
        in_specs=[vmem],
        out_specs=vmem,
        compiler_params=large,
        name="solve_part",
    )(rows)
    return (step, white)


def solution(mesh):
    in_specs = (
        P(None, AXES),
        P(None, AXES),
        P(None, AXES),
        P(None, AXES),
        P(AXES, None),
        P(AXES, None),
        P(),
    )
    out_specs = (P(), P(None, AXES))
    return jax.shard_map(body, mesh=mesh, in_specs=in_specs, out_specs=out_specs, check_vma=False)
```

time: 117 us -> 101 us (0.86)
  between operations: 14.1 us -> 0.69 us
  waiting for transfers between devices: 9.24 us -> 2.21 us
  local copies, waits for them, and re-layouts: 9.98 us -> 3.15 us
  blocking collectives: 15.2 us -> 19.9 us
  Pallas kernels: 48.2 us -> 51.7 us
  starting transfers between devices: 20.2 us -> 23.2 us
    all_to_all x1 -> x2, starting transfers between devices: 9.52 us -> 17.1 us  [the longest x1 9.53 us: body(): table = lax.all_to_all(request, AXES, 0, 0, tiled=True)]
    ppermute x2 -> x1, waiting for transfers between devices: 5.38 us -> 0.01 us  [passed_along(): return lax.ppermute(block, axis, route)]
    all_to_all x1, blocking collectives: 15.2 us -> 19.9 us  [body(): rows = lax.all_to_all(row, AXES, 0, 0, tiled=True)]
    ppermute x2 -> x1, starting transfers between devices: 8.05 us -> 3.95 us  [shifted(): lax.ppermute(value, axis, [(source, source + steps) for source in range(f...]
    unnamed x16 -> x8, local copies, waits for them, and re-layouts: 7.14 us -> 3.15 us
    pallas_call x3 -> x6, Pallas kernels: 48.2 us -> 51.7 us  [the longest x1 32.2 us: body(): pl.pallas_call(first_kernel, out_shape=(shape(B, N), shape(6 * B, LEAD),...]
    all_gather x1 -> x0, waiting for transfers between devices: 3.17 us -> none  [body(): every = lax.all_gather(coarse_values.T, AXES, axis=0, tiled=True)]
    all_to_all x1 -> x2, waiting for transfers between devices: 0.01 us -> 2.21 us  [the longest x1 2.21 us: body(): table = lax.all_to_all(request, AXES, 0, 0, tiled=True)]
  transfers between devices with their start and end apart: 6 -> 4, of which waited for: 2 -> 1; matrix products, arithmetic and copies ran while one was open for 1% -> 0% of each run, Pallas kernels for 35% -> 38%
where the time goes in v2:
time: 101 us
  Pallas kernels  51.7 us (51%)
  starting transfers between devices  23.2 us (23%)
  blocking collectives  19.9 us (20%)
  local copies, waits for them, and re-layouts  3.15 us (3%)
  waiting for transfers between devices  2.21 us (2%)
    pallas_call x1, Pallas kernels, body(): pl.pallas_call(first_kernel, out_shape=(shape(B, N), shape(6 * B, LEAD),...  32.2 us
    all_to_all x1, blocking collectives, body(): rows = lax.all_to_all(row, AXES, 0, 0, tiled=True)  19.9 us
    all_to_all x1, starting transfers between devices, body(): table = lax.all_to_all(request, AXES, 0, 0, tiled=True)  9.53 us
    all_to_all x1, starting transfers between devices, body(): arrived = lax.all_to_all(send, AXES, 0, 0, tiled=True)  7.56 us
    pallas_call x1, Pallas kernels, body(): pl.pallas_call(second_kernel, out_shape=(shape(reps, B), shape(devices, B...  6.76 us
    pallas_call x1, Pallas kernels, body(): pl.pallas_call(fine_kernel, out_shape=(shape(B, B), shape(8, 2 * B)), in_...  6.09 us
    ppermute x1, starting transfers between devices, shifted(): lax.ppermute(value, axis, [(source, source + steps) for source in range(f...  3.95 us
    unnamed x8, local copies, waits for them, and re-layouts  3.15 us
  transfers between devices with their start and end apart: 4, of which 1 were waited for; matrix products, arithmetic and copies ran while one was open for 0% of the time, Pallas kernels for 38%

profile of v2, /device:TPU:1, one launch (start us, length us, event | category | flops | bytes accessed | tf_op | source)
XLA Modules:
  0.0 100.9 jit_solution(2883267779435561759)
XLA Ops:
  0.6 2.0 %request_part.1 = (f32[128,128]{1,0:T(8,128)}, s32[1,384]{1,0:T(1,128)}, f32[520,128]{1,0:T(8,128)}) custom-call(f32[4,16]{1,0:T(4,128)} %coarse_coords.1, s32[1,384]{1,0:T(1,128)} %coarse.3, f32[4,128]{1,0:T(4,128)} %own.2, f32[512,128]{1,0:T(8,128)} %own.3), custom_call_target="tpu_custom_call" | custom-call | tf_op jit(solution)/shard_map/request_part/pallas_call | solution.py:337
  2.7 2.1 %collective-permute-start.1 = (f32[520,128]{1,0:T(8,128)}, f32[520,128]{1,0:T(8,128)S(1)}, u32[]{:S(2)}, u32[]{:S(2)}) collective-permute-start(f32[520,128]{1,0:T(8,128)} %get-tuple-element.14), channel_id=1, source_target_pairs={{15,0},{0,1},{1,2},{2,3},{3,4},{4,5},{5,6},{6,7},{7,8},{8,9},{9,10... | collective-permute-start | bytes 798728 | tf_op jit(solution)/shard_map/ppermute | solution.py:37
  4.8 3.9 %collective-permute-start = (f32[520,128]{1,0:T(8,128)}, f32[520,128]{1,0:T(8,128)S(1)}, u32[]{:S(2)}, u32[]{:S(2)}) collective-permute-start(f32[520,128]{1,0:T(8,128)} %get-tuple-element.14), channel_id=1, source_target_pairs={{0,16},{16,32},{32,48},{48,64},{64,80},{80,96},{96,112},{1,17},{17... | collective-permute-start | bytes 798728 | tf_op jit(solution)/shard_map/ppermute | solution.py:31
  8.7 9.5 %all-to-all-start = ((f32[128,1,128]{2,1,0:T(1,128)}), f32[128,1,128]{2,1,0:T(1,128)S(1)}, u32[]{:S(2)}, u32[]{:S(2)}) async-start(f32[128,1,128]{2,1,0:T(1,128)} %bitcast.16), calls=%async_computation | async-start | bytes 131072 | tf_op jit(solution)/shard_map/all_to_all | solution.py:347
  18.3 0.0 collective-permute-done.1.left
  18.3 0.0 copy-start.1
  18.3 0.0 collective-permute-done.up
  18.3 0.7 copy-done.1
  19.0 0.0 copy-start.2
  19.0 0.7 copy-done.2
  19.7 6.1 %fine_part.1 = (f32[128,128]{1,0:T(8,128)}, f32[8,256]{1,0:T(8,128)}) custom-call(f32[6]{0:T(128)} %theta.3, f32[520,128]{1,0:T(8,128)} %copy-done.2, f32[520,128]{1,0:T(8,128)} %copy-done.1, f32[4,128]{1,0:T(4,128)} %own.2, s32[1,128]{1,0:T(1,128)} %fine.3), custom_call_target="tpu_custom_call" | custom-call | flops 4000000000 | bytes 1048576 | tf_op jit(solution)/shard_map/fine_part/pallas_call | solution.py:348
  25.8 2.2 %all-to-all-done = f32[128,1,128]{2,1,0:T(1,128)S(1)} async-done(((f32[128,1,128]{2,1,0:T(1,128)}), f32[128,1,128]{2,1,0:T(1,128)S(1)}, u32[]{:S(2)}, u32[]{:S(2)}) %all-to-all-start) | async-done | bytes 65568 | tf_op jit(solution)/shard_map/all_to_all | solution.py:347
  28.0 0.0 copy-start.3
  28.0 0.6 copy-done.3
  28.6 2.5 %send_part.1 = f32[3072,128]{1,0:T(8,128)} custom-call(f32[128,128]{1,0:T(8,128)} %bitcast.13, f32[16,512]{1,0:T(8,128)} %bitcast.18, f32[8,256]{1,0:T(8,128)} %get-tuple-element.15.after.lines), custom_call_target="tpu_custom_call" | custom-call | tf_op jit(solution)/shard_map/send_part/pallas_call | solution.py:357
  31.1 7.6 %all-to-all-start.1 = ((f32[128,24,128]{2,1,0:T(8,128)}), f32[128,24,128]{2,1,0:T(8,128)S(1)}, u32[]{:S(2)}, u32[]{:S(2)}) async-start(f32[128,24,128]{2,1,0:T(8,128)} %bitcast.11), calls=%async_computation.1 | async-start | bytes 3145728 | tf_op jit(solution)/shard_map/all_to_all | solution.py:365
  38.7 32.2 %fisher_part.1 = (f32[128,640]{1,0:T(8,128)}, f32[768,512]{1,0:T(8,128)}, f32[768,128]{1,0:T(8,128)}, f32[32,128]{1,0:T(8,128)}) custom-call(f32[6]{0:T(128)} %theta.3, f32[128,128]{1,0:T(8,128)} %bitcast.14, f32[8,256]{1,0:T(8,128)} %get-tuple-element.15.after.lines, f32[128,128]{1,0:T(8,128)} %get-tuple-element.17.d_fine, s32[1,384]{1,0:T(1,128)} %coarse.3), custom_call_target="tpu_custom_call" | custom-call | flops 30000001024 | bytes 1048576 | tf_op jit(solution)/shard_map/fisher_part/pallas_call | solution.py:366
  70.9 0.0 all-to-all-done.1
  70.9 0.0 copy-start
  70.9 1.1 %copy-done = f32[128,24,128]{2,1,0:T(8,128)} copy-done((f32[128,24,128]{2,1,0:T(8,128)}, f32[128,24,128]{2,1,0:T(8,128)S(1)}, u32[]{:S(2)}) %copy-start) | copy-done | bytes 1572888
  72.0 6.8 %gradient_part.1 = (f32[512,128]{1,0:T(8,128)}, f32[128,128]{1,0:T(8,128)}) custom-call(f32[3072,128]{1,0:T(8,128)} %bitcast.12, s32[1,384]{1,0:T(1,128)} %get-tuple-element.16.place, f32[520,128]{1,0:T(8,128)} %copy-done.2, f32[520,128]{1,0:T(8,128)} %copy-done.1, f32[512,128]{1,0:T(8,128)} %own.3, s32[1,128]{1,0:T(1,128)} %fine.3, ...), custom_call_target="tpu_custom_call" | custom-call | tf_op jit(solution)/shard_map/gradient_part/pallas_call | solution.py:387
  78.8 19.9 %all_to_all.33 = f32[128,1,128]{2,1,0:T(1,128)} all-to-all(f32[128,1,128]{2,1,0:T(1,128)} %bitcast.17), channel_id=1, replica_groups=mesh['row'=8,'col'=16] {'row','col'}, dimensions={0} | all-to-all | bytes 131072 | tf_op jit(solution)/shard_map/all_to_all | solution.py:396
  98.7 2.2 %solve_part.1 = f32[6]{0:T(128)} custom-call(f32[128,128]{1,0:T(8,128)} %bitcast.15), custom_call_target="tpu_custom_call" | custom-call | tf_op jit(solution)/shard_map/solve_part/pallas_call | solution.py:397
Async XLA Ops:
  2.7 15.6 %collective-permute-start.1 = (f32[520,128]{1,0:T(8,128)}, f32[520,128]{1,0:T(8,128)S(1)}, u32[]{:S(2)}, u32[]{:S(2)}) collective-permute-start(f32[520,128]{1,0:T(8,128)} %get-tuple-element.14), channel_id=1, source_target_pairs={{15,0},{0,1},{1,2},{2,3},{3,4},{4,5},{5,6},{6,7},{7,8},{8,9},{9,10... | collective-permute-start | bytes 798728 | tf_op jit(solution)/shard_map/ppermute | solution.py:37
  4.8 13.5 %collective-permute-start = (f32[520,128]{1,0:T(8,128)}, f32[520,128]{1,0:T(8,128)S(1)}, u32[]{:S(2)}, u32[]{:S(2)}) collective-permute-start(f32[520,128]{1,0:T(8,128)} %get-tuple-element.14), channel_id=1, source_target_pairs={{0,16},{16,32},{32,48},{48,64},{64,80},{80,96},{96,112},{1,17},{17... | collective-permute-start | bytes 798728 | tf_op jit(solution)/shard_map/ppermute | solution.py:31
  8.7 19.2 %all-to-all-start = ((f32[128,1,128]{2,1,0:T(1,128)}), f32[128,1,128]{2,1,0:T(1,128)S(1)}, u32[]{:S(2)}, u32[]{:S(2)}) async-start(f32[128,1,128]{2,1,0:T(1,128)} %bitcast.16), calls=%async_computation | async-start | bytes 131072 | tf_op jit(solution)/shard_map/all_to_all | solution.py:347
  18.3 0.7 copy-start.1
  19.0 0.7 copy-start.2
  28.0 0.6 copy-start.3
  31.1 39.8 %all-to-all-start.1 = ((f32[128,24,128]{2,1,0:T(8,128)}), f32[128,24,128]{2,1,0:T(8,128)S(1)}, u32[]{:S(2)}, u32[]{:S(2)}) async-start(f32[128,24,128]{2,1,0:T(8,128)} %bitcast.11), calls=%async_computation.1 | async-start | bytes 3145728 | tf_op jit(solution)/shard_map/all_to_all | solution.py:365
  70.9 1.1 %copy-start = (f32[128,24,128]{2,1,0:T(8,128)}, f32[128,24,128]{2,1,0:T(8,128)S(1)}, u32[]{:S(2)}) copy-start(f32[128,24,128]{2,1,0:T(8,128)S(1)} %all-to-all-done.1) | copy-start | bytes 4718596

commit v3 on v2

v3 whole, which is shorter than its diff:
```python
import math

import jax
import jax.numpy as jnp
from jax import lax
from jax.experimental import pallas as pl
from jax.experimental.pallas import tpu as pltpu
from jax.sharding import PartitionSpec as P

HIGH = lax.Precision.HIGHEST
ROOT_FIVE = math.sqrt(5.0)
NUGGET = 0.2
RANGE_BASE = 0.5
F32 = jnp.float32
BF16 = jnp.bfloat16
AXES = ("row", "col")

B = 128
N = 640
LEAD = 512
COARSE = 384
HALF = 64
CP = 16
MOST = 6
FINE, PLACE, WANTED, SPREAD, VARIANCE, NUG, TAIL = 4, 5, 8, 11, 15, 16, 24
MROW, PROW, FIELDS = 768, 896, 928


def shifted(value, axis, steps):
    count = lax.axis_size(axis)
    first, last = (max(0, -steps), min(count, count - steps))
    return lax.ppermute(value, axis, [(source, source + steps) for source in range(first, last)])


def passed_along(block, axis, distance):
    devices = range(lax.axis_size(axis))
    route = [((i - distance) % len(devices), i) for i in devices]
    return lax.ppermute(block, axis, route)


def nn(a, b, precision=HIGH):
    return lax.dot_general(a, b, (((1,), (0,)), ((), ())), precision=precision, preferred_element_type=F32)


def nt(a, b, precision=HIGH):
    return lax.dot_general(a, b, (((1,), (1,)), ((), ())), precision=precision, preferred_element_type=F32)


def tn(a, b, precision=HIGH):
    return lax.dot_general(a, b, (((0,), (0,)), ((), ())), precision=precision, preferred_element_type=F32)


def iota(shape, dim):
    return lax.broadcasted_iota(jnp.int32, shape, dim)


def halves(x):
    high = x.astype(BF16)
    return high, (x - high.astype(F32)).astype(BF16)


def thirds(x):
    high = x.astype(BF16)
    rest = x - high.astype(F32)
    mid = rest.astype(BF16)
    return high, mid, (rest - mid.astype(F32)).astype(BF16)


def picked(table, one_hot, dot):
    high, mid, low = thirds(table)
    return (dot(high, one_hot, None) + dot(mid, one_hot, None)) + dot(low, one_hot, None)


def six_left(x):
    one, two, three = thirds(x)
    return jnp.concatenate([one, one, two, two, one, three], axis=1)


def six_right(x):
    one, two, three = thirds(x)
    return jnp.concatenate([one, two, one, two, three, one], axis=0)


def three_terms(left, right, dot):
    rows = left[0].shape[0]
    both = dot(jnp.concatenate(left, axis=0), right[0], None)
    return (both[:rows] + both[rows:]) + dot(left[0], right[1], None)


def wide(x, j):
    return jnp.broadcast_to(x[:, j : j + 1], (8, B))


def tall(x, k):
    return jnp.broadcast_to(x[k : k + 1, :], (8, B))


def inverse_factor(s):
    tiles = B // 8
    s = list(s)
    sub, lane = iota((8, B), 0), iota((8, B), 1)
    out = []
    ahead = [wide(s[0], j) for j in range(8)]
    for g in range(tiles):
        k0 = 8 * g
        live = range(g, tiles)
        cols = [{v: wide(s[v], k0 + j) for v in range(g + 1, tiles)} for j in range(8)]
        for j in range(8):
            cols[j][g] = ahead[j]
        if g + 1 < tiles:
            ahead = [wide(s[g + 1], k0 + 8 + j) for j in range(8)]
        inside = (lane >= k0) & (lane < k0 + 8)
        s[g] = jnp.where(inside, (lane == sub + k0).astype(F32), s[g])
        for v in range(g + 1, tiles):
            s[v] = jnp.where(inside, 0.0, s[v])
        pivots = jnp.ones((8, B), F32)
        pivot = tall(cols[0][g], 0)
        for k in range(8):
            col = cols[k]
            pivots = jnp.where(sub == k, pivot, pivots)
            over = 1.0 / pivot
            if k < 7:
                below = tall(col[g], k + 1)
                pivot = tall(cols[k + 1][g], k + 1) - (below * below) * over
            factor = {v: col[v] * over for v in live}
            factor[g] = jnp.where(sub > k, factor[g], 0.0)
            for later in range(k + 1, 8):
                at = tall(col[g], later)
                for v in live:
                    cols[later][v] = cols[later][v] - factor[v] * at
            if g + 1 < tiles:
                for j in range(8):
                    ahead[j] = ahead[j] - factor[g + 1] * tall(col[g + 1], j)
            row = tall(s[g], k)
            for v in live:
                s[v] = s[v] - factor[v] * row
        root = lax.rsqrt(pivots)
        root = root * (1.5 - 0.5 * pivots * root * root)
        out.append(jnp.where(lane <= sub + k0, s[g] * root, 0.0))
    return out


def request_kernel(theta, coarse_coords, coarse, coords, values, fine, out_ref, tile_ref):
    reps = values.shape[0]
    tile, slot = coarse[...] // CP, coarse[...] % CP
    hot = (iota((B, COARSE), 0) == tile).astype(BF16)
    earlier = (iota((COARSE, COARSE), 0) < iota((COARSE, COARSE), 1)).astype(BF16)
    rank = jnp.sum(hot.astype(F32) * nn(hot, earlier, None), axis=0, keepdims=True).astype(jnp.int32)
    asked = jnp.where(iota((B, COARSE), 0) == rank + 4 * CP, slot, 0).astype(F32).astype(BF16)
    line = jnp.concatenate([coarse_coords[k : k + 1, :] for k in range(4)] + [jnp.zeros((1, B - 4 * CP), F32)], axis=1)
    out_ref[...] = line + nt(hot, asked, None)
    place = (tile * MOST + rank).astype(F32)
    wanted = coarse[...].astype(F32)
    rows = [coords[...], fine[...].astype(F32)]
    rows += [place[:, c * B : (c + 1) * B] for c in range(COARSE // B)]
    rows += [wanted[:, c * B : (c + 1) * B] for c in range(COARSE // B)]
    rows += [jnp.exp(jnp.full((1, B), theta[1 + k], F32)) * RANGE_BASE for k in range(4)]
    rows += [jnp.exp(jnp.full((1, B), theta[0], F32)), NUGGET * jnp.exp(jnp.full((1, B), theta[5], F32))]
    rows += [jnp.zeros((TAIL - NUG - 1, B), F32)]
    tile_ref[:reps, :] = values[...]
    tile_ref[reps:, :] = jnp.concatenate(rows, axis=0)


def send_kernel(table, coarse_values, after, send_ref):
    del after
    three = jnp.concatenate(thirds(coarse_values[...]), axis=0)
    slots = (iota((B, 3 * CP), 1) % CP).astype(F32)
    chunks = coarse_values.shape[1] // B
    for r in range(MOST):
        hot = (table[:, 4 * CP + r : 4 * CP + r + 1] == slots).astype(BF16)
        rows = nn(hot, three, None)
        for c in range(chunks):
            send_ref[pl.ds(r * chunks + c, B, stride=MOST * chunks), :] = rows[:, c * B : (c + 1) * B]


def pair(down, across, variance, live_down, live_across):
    squares = []
    for k in range(4):
        gap = down[:, k : k + 1] - across[k]
        squares.append(gap * gap)
    root = ROOT_FIVE * jnp.sqrt((squares[0] + squares[1]) + (squares[2] + squares[3]))
    paired = (live_down * live_across) * (variance * jnp.exp(-root))
    return paired * (1.0 + root + root * root * (1.0 / 3.0)), paired * ((5.0 / 3.0) * (1.0 + root)), squares


def fine_kernel(tile, up, left, out_ref):
    reps = tile.shape[0] - TAIL
    tail = tile[reps:, :]
    fine = tail[FINE : FINE + 1, :]
    column = iota((B, HALF), 0).astype(F32)
    up_hot = (column == fine[:, :HALF]).astype(BF16)
    left_hot = (column == fine[:, HALF:]).astype(BF16)
    upper_live = (lax.axis_index("row") > 0).astype(F32)
    picks = jnp.concatenate(
        [picked(up[reps : reps + 8, :], up_hot, nn) * upper_live, picked(left[reps : reps + 8, :], left_hot, nn)], axis=1
    )
    across = [picks[k : k + 1] / tail[SPREAD + k : SPREAD + k + 1] for k in range(4)]
    live = jnp.where(iota((1, B), 1) < HALF, upper_live, 1.0)
    lines = jnp.concatenate(across + [live, jnp.zeros((3, B), F32)], axis=0)
    own_lines = [tail[k : k + 1, :] / tail[SPREAD + k : SPREAD + k + 1] for k in range(4)]
    own_lines = jnp.concatenate(own_lines + [jnp.ones((1, B), F32), jnp.zeros((3, B), F32)], axis=0)
    thrice = jnp.concatenate([tail[SPREAD : NUG + 1, :]] * 3, axis=1)
    ends = [jnp.concatenate([tail[n + c : n + c + 1, :] for c in range(3)], axis=1) for n in (PLACE, WANTED)]
    out_ref[2 * B :, :] = jnp.concatenate([lines, own_lines, jnp.concatenate(ends + [thrice], axis=0)], axis=1)
    down = jnp.concatenate([lines, jnp.zeros((B - 8, B), F32)], axis=0).T
    kernel, _, _ = pair(down, across, tail[VARIANCE : VARIANCE + 1, :], down[:, 4:5], live)
    same = iota((B, B), 0) == iota((B, B), 1)
    cov = kernel + jnp.where(same, live * tail[NUG : NUG + 1, :] + 1.0 - live, 0.0)
    tiles = inverse_factor([cov[8 * v : 8 * (v + 1)] for v in range(B // 8)])
    for v in range(B // 8):
        out_ref[8 * v : 8 * (v + 1), reps:] = tiles[v]
    hot = (jnp.broadcast_to(fine, (B, B)).T == iota((B, B), 1).astype(F32)).astype(BF16)
    out_ref[:HALF, :reps] = picked2(hot[:HALF], up[:reps, :])
    out_ref[HALF:B, :reps] = picked2(hot[HALF:], left[:reps, :])
    out_ref[B : 2 * B, :reps] = tile[:reps, :].T
    out_ref[B : 2 * B, reps:] = jnp.zeros((B, B), F32)


def first_kernel(table, given, out_ref, k_ref, s_ref, d_ref, u_ref, left_ref, right_ref, f_ref, f3_ref, y_ref):
    lines = given[2 * B :, : 2 * B]
    ends = given[2 * B :, 2 * B :]
    wanted = ends[1:2].astype(jnp.int32)
    tile_hot = (iota((B, COARSE), 0) == wanted // CP).astype(BF16)
    rows = picked(table[:, : 4 * CP], tile_hot, tn)
    rows = jnp.where((iota((4 * CP, COARSE), 0) % CP) == wanted % CP, rows, 0.0)
    across = []
    for k in range(4):
        line = jnp.sum(rows[k * CP : (k + 1) * CP], axis=0, keepdims=True) / ends[2 + k : 3 + k]
        across.append(jnp.concatenate([lines[k : k + 1, :B], line, lines[k : k + 1, B:]], axis=1))
    live = jnp.concatenate([lines[4:5, :B], jnp.ones((1, N - B), F32)], axis=1)
    down = jnp.concatenate(across + [live] + [jnp.zeros((B - 5, N), F32)], axis=0).T
    variance = jnp.concatenate([ends[6:7], ends[6:7, : N - COARSE]], axis=1)
    nugget = jnp.concatenate([ends[7:8], ends[7:8, : N - COARSE]], axis=1)
    out_ref[FIELDS : FIELDS + 2 * B, :LEAD] = given[: 2 * B, :LEAD]
    out_ref[FIELDS:, LEAD:] = jnp.broadcast_to(ends[0:1], (B, COARSE)).T
    for r in range(N // B):
        here = slice(r * B, (r + 1) * B)
        kernel, common, squares = pair(down[here], across, variance, down[here, 4:5], live)
        for i, part in enumerate([kernel] + [common * square for square in squares]):
            there = slice(i * N, (i + 1) * N)
            f_ref[here, there], f_ref[N + r * B : N + (r + 1) * B, there], f3_ref[here, there] = thirds(part)
        same = iota((B, N), 0) + r * B == iota((B, N), 1)
        k_ref[here, :] = kernel + jnp.where(same, live * nugget + 1.0 - live, 0.0)

    def conditional(p):
        at = pl.multiple_of(p * B, B)
        after = pl.multiple_of(p * B + B, B)
        u = nn(six_left(d_ref[...]), six_right(k_ref[pl.ds(at, B), pl.ds(after, B)]), None)
        s_ref[...] = k_ref[pl.ds(after, B), pl.ds(after, B)] - nn(six_left(u.T), six_right(u), None)

    d_ref[...] = given[:B, LEAD:]
    conditional(0)

    def sweep(p, carry):
        tiles = inverse_factor([s_ref[8 * v : 8 * (v + 1), :] for v in range(B // 8)])
        last = pl.multiple_of(p * B - B, B)
        d = d_ref[...]
        u_ref[...] = nn(six_left(d), six_right(k_ref[pl.ds(last, B), :]), None)
        u_ref[:, pl.ds(last, B)] = -d
        k_ref[pl.ds(last, B), :] = jnp.zeros((B, N), F32)
        k_ref[:, pl.ds(last, B)] = jnp.zeros((N, B), F32)
        left_ref[...] = six_left(u_ref[...].T)
        right_ref[...] = six_right(u_ref[...])
        k_ref[...] -= nn(left_ref[...], right_ref[...], None)
        for v in range(B // 8):
            d_ref[8 * v : 8 * (v + 1), :] = tiles[v]

        @pl.when(p < N // B - 1)
        def _():
            conditional(p)

        return carry

    lax.fori_loop(1, N // B, sweep, 0)
    d = d_ref[...]
    out_ref[MROW : MROW + B, :LEAD] = -nt(d, k_ref[:LEAD, LEAD:])
    out_ref[MROW : MROW + B, LEAD:] = d
    m = out_ref[MROW : MROW + B, :]
    parts = halves(m)
    twice = jnp.concatenate([jnp.concatenate([part, part], axis=1) for part in parts], axis=0)
    large = nn(twice, f_ref[...], None)
    small = large[B:] + nn(parts[0], f3_ref[...], None)
    for i in range(5):
        there = slice(i * N, (i + 1) * N)
        y_ref[i * B : (i + 1) * B, :] = large[:B, there] + small[:, there]
    y_ref[5 * B :, :] = m * (live * nugget)
    high, low = halves(y_ref[...])
    out_ref[:MROW, :LEAD] = -three_terms((high[:, :LEAD], low[:, :LEAD]), halves(k_ref[:LEAD, :LEAD]), nn)
    out_ref[:MROW, LEAD:] = three_terms((high, low), parts, nt)

    def folded(x):
        x = jnp.sum(x.reshape(B // 8, 8, x.shape[1]), axis=0)
        total = x[:, :B]
        for c in range(1, x.shape[1] // B):
            total = total + x[:, c * B : (c + 1) * B]
        return total

    sums = []
    for i in range(6):
        for j in range(i + 1):
            lead_part = out_ref[i * B : (i + 1) * B, :LEAD] * y_ref[j * B : (j + 1) * B, :LEAD]
            own_part = out_ref[i * B : (i + 1) * B, LEAD:] * out_ref[j * B : (j + 1) * B, LEAD:]
            sums.append(jnp.sum(2.0 * folded(lead_part) + folded(own_part), axis=0, keepdims=True))
    for i in range(6):
        sums.append(jnp.sum(folded(y_ref[i * B : (i + 1) * B, :] * m), axis=0, keepdims=True))
    sums.append(jnp.zeros((5, B), F32))
    out_ref[PROW:FIELDS, :B] = jnp.concatenate(sums, axis=0)


def picked2(one_hot, table):
    high, low = halves(table)
    return nt(one_hot, high, None) + nt(one_hot, low, None)


def second_kernel(arrived, parts, white_ref, row_ref, v_ref, given, sems):
    pieces = ((FIELDS, FIELDS + COARSE), (MROW, FIELDS), (0, MROW))
    copies = [
        pltpu.make_async_copy(parts.at[first:end], given.at[first:end], sems.at[n]) for n, (first, end) in enumerate(pieces)
    ]
    for copy in copies:
        copy.start()
    copies[0].wait()
    reps = white_ref.shape[0]
    chunks = reps // B
    held = arrived.shape[0] // chunks
    v_ref[:B, :] = given[FIELDS : FIELDS + B, :reps]
    v_ref[LEAD:, :] = given[FIELDS + B : FIELDS + 2 * B, :reps]
    hot = (given[FIELDS:, LEAD : LEAD + 1] == iota((COARSE, held), 1).astype(F32)).astype(BF16)
    for c in range(chunks):
        high, low = halves(arrived[pl.ds(c, held, stride=chunks), :])
        v_ref[B:LEAD, c * B : (c + 1) * B] = nn(hot, high, None) + nn(hot, low, None)
    copies[1].wait()
    white = nn(given[MROW : MROW + B, :], v_ref[...])
    white_ref[...] = white.T
    cross = nt(white, v_ref[:LEAD, :])
    square = nt(white, white)
    copies[2].wait()
    part = given[PROW:FIELDS, :B]
    lines = []
    for i in range(6):
        both = given[i * B : (i + 1) * B, :LEAD] * cross
        both = (both[:, :B] + both[:, B : 2 * B]) + (both[:, 2 * B : 3 * B] + both[:, 3 * B :])
        both = both + 0.5 * (given[i * B : (i + 1) * B, LEAD:] * square)
        lines.append(jnp.sum(both, axis=0, keepdims=True) - (0.5 * reps) * part[21 + i : 22 + i, :])
    whole = jnp.concatenate([(0.5 * reps) * part[:21, :]] + lines + [jnp.zeros((B - 27, B), F32)], axis=0)
    row_ref[...] = jnp.broadcast_to(jnp.sum(whole.T, axis=0, keepdims=True), row_ref.shape)


def third_kernel(rows, step_ref):
    total = jnp.broadcast_to(jnp.sum(rows[...], axis=0, keepdims=True), (8, B))
    sub, lane = iota((8, B), 0), iota((8, B), 1)
    a = jnp.zeros((8, B), F32)
    for i in range(6):
        for j in range(6):
            low, high = min(i, j), max(i, j)
            entry = jnp.broadcast_to(total[:, high * (high + 1) // 2 + low : high * (high + 1) // 2 + low + 1], (8, B))
            a = jnp.where((sub == i) & (lane == j), entry, a)
        entry = jnp.broadcast_to(total[:, 21 + i : 22 + i], (8, B))
        a = jnp.where((sub == i) & (lane == 6), entry, a)
    for k in range(6):
        row = jnp.broadcast_to(a[k : k + 1, :], (8, B))
        col = jnp.broadcast_to(a[:, k : k + 1], (8, B))
        row = row / jnp.broadcast_to(row[:, k : k + 1], (8, B))
        a = jnp.where(sub == k, row, a - col * row)
    step_ref[...] = jnp.sum(jnp.where((lane == sub) & (sub < 6), jnp.broadcast_to(a[:, 6:7], (8, B)), 0.0), axis=0)[:6]


def body(coords, values, coarse_coords, coarse_values, fine_index, coarse_index, log_params):
    reps = values.shape[0]
    devices = lax.axis_size("row") * lax.axis_size("col")
    vmem = pl.BlockSpec(memory_space=pltpu.VMEM)
    smem = pl.BlockSpec(memory_space=pltpu.SMEM)

    def shape(*dims):
        return jax.ShapeDtypeStruct(dims, F32)

    def cost(flops):
        return pl.CostEstimate(flops=flops, bytes_accessed=2**20, transcendentals=0)

    def room(mib):
        return pltpu.CompilerParams(vmem_limit_bytes=mib * 2**20)

    request, tile = pl.pallas_call(
        request_kernel,
        out_shape=(shape(devices, B), shape(reps + TAIL, B)),
        in_specs=[smem] + [vmem] * 5,
        out_specs=(vmem,) * 2,
        compiler_params=room(60),
        name="request_part",
    )(log_params, coarse_coords, coarse_index, coords, values, fine_index)
    up = shifted(tile, "row", 1)
    left = passed_along(tile, "col", 1)
    table = lax.all_to_all(request, AXES, 0, 0, tiled=True)
    fine = pl.pallas_call(
        fine_kernel,
        out_shape=shape(2 * B + 8, N),
        in_specs=[vmem] * 3,
        out_specs=vmem,
        compiler_params=room(8),
        cost_estimate=cost(4 * 10**9),
        name="fine_part",
    )(tile, up, left)
    send = pl.pallas_call(
        send_kernel,
        out_shape=shape(devices * MOST * reps // B, B),
        in_specs=[vmem] * 2 + [pl.BlockSpec(memory_space=pl.ANY)],
        out_specs=vmem,
        compiler_params=room(8),
        name="send_part",
    )(table, coarse_values.T, fine)
    arrived = lax.all_to_all(send, AXES, 0, 0, tiled=True)
    parts = pl.pallas_call(
        first_kernel,
        out_shape=shape(FIELDS + COARSE, N),
        in_specs=[vmem] * 2,
        out_specs=vmem,
        scratch_shapes=[
            pltpu.VMEM((N, N), F32),
            pltpu.VMEM((B, B), F32),
            pltpu.VMEM((B, B), F32),
            pltpu.VMEM((B, N), F32),
            pltpu.VMEM((N, 6 * B), BF16),
            pltpu.VMEM((6 * B, N), BF16),
            pltpu.VMEM((2 * N, 5 * N), BF16),
            pltpu.VMEM((N, 5 * N), BF16),
            pltpu.VMEM((6 * B, N), F32),
        ],
        compiler_params=room(36),
        cost_estimate=cost(30 * 10**9),
        name="fisher_part",
    )(table, fine)
    white, row = pl.pallas_call(
        second_kernel,
        out_shape=(shape(reps, B), shape(devices, B)),
        in_specs=[vmem, pl.BlockSpec(memory_space=pl.ANY)],
        out_specs=(vmem,) * 2,
        scratch_shapes=[
            pltpu.VMEM((N, reps), F32),
            pltpu.VMEM((FIELDS + COARSE, N), F32),
            pltpu.SemaphoreType.DMA((3,)),
        ],
        compiler_params=room(24),
        name="gradient_part",
    )(arrived, parts)
    rows = lax.all_to_all(row, AXES, 0, 0, tiled=True)
    step = pl.pallas_call(
        third_kernel,
        out_shape=shape(6),
        in_specs=[vmem],
        out_specs=vmem,
        compiler_params=room(8),
        name="solve_part",
    )(rows)
    return (step, white)


def solution(mesh):
    in_specs = (
        P(None, AXES),
        P(None, AXES),
        P(None, AXES),
        P(None, AXES),
        P(AXES, None),
        P(AXES, None),
        P(),
    )
    out_specs = (P(), P(None, AXES))
    return jax.shard_map(body, mesh=mesh, in_specs=in_specs, out_specs=out_specs, check_vma=False)
```

time: 101 us -> 90.4 us (0.90)
  Pallas kernels: 51.7 us -> 40.1 us
  starting transfers between devices: 23.2 us -> 20 us
  waiting for transfers between devices: 2.21 us -> 5.36 us
  local copies, waits for them, and re-layouts: 3.15 us -> 4.6 us
    pallas_call x3, Pallas kernels: 40.3 us -> 31.5 us  [the longest x1 26.1 us: body(): pl.pallas_call(first_kernel, out_shape=shape(FIELDS + COARSE, N), in_spec...]
    all_to_all x1, waiting for transfers between devices: 2.21 us -> 5.35 us  [body(): table = lax.all_to_all(request, AXES, 0, 0, tiled=True)]
    all_to_all x1, starting transfers between devices: 7.56 us -> 4.44 us  [body(): arrived = lax.all_to_all(send, AXES, 0, 0, tiled=True)]
    unnamed x8, local copies, waits for them, and re-layouts: 3.15 us -> 4.6 us
    pallas_call x1, Pallas kernels: 6.76 us -> 5.59 us  [body(): pl.pallas_call(second_kernel, out_shape=(shape(reps, B), shape(devices, B...]
  transfers between devices with their start and end apart: 4 -> 4, of which waited for: 1 -> 1; matrix products, arithmetic and copies ran while one was open for 0% -> 0% of each run, Pallas kernels for 38% -> 33%
where the time goes in v3:
time: 90.4 us; the launch traced here: 90.1 us
  Pallas kernels  40.1 us (44%)
  starting transfers between devices  20 us (22%)
  blocking collectives  19.3 us (21%)
  waiting for transfers between devices  5.36 us (6%)
  local copies, waits for them, and re-layouts  4.6 us (5%)
    pallas_call x1, Pallas kernels, body(): pl.pallas_call(first_kernel, out_shape=shape(FIELDS + COARSE, N), in_spec...  26.1 us
    all_to_all x1, blocking collectives, body(): rows = lax.all_to_all(row, AXES, 0, 0, tiled=True)  19.3 us
    all_to_all x1, starting transfers between devices, body(): table = lax.all_to_all(request, AXES, 0, 0, tiled=True)  9.52 us
    pallas_call x1, Pallas kernels, body(): pl.pallas_call(second_kernel, out_shape=(shape(reps, B), shape(devices, B...  5.59 us
    all_to_all x1, waiting for transfers between devices, body(): table = lax.all_to_all(request, AXES, 0, 0, tiled=True)  5.35 us
    unnamed x8, local copies, waits for them, and re-layouts  4.6 us
    all_to_all x1, starting transfers between devices, body(): arrived = lax.all_to_all(send, AXES, 0, 0, tiled=True)  4.44 us
    ppermute x1, starting transfers between devices, shifted(): lax.ppermute(value, axis, [(source, source + steps) for source in range(f...  3.95 us
  transfers between devices with their start and end apart: 4, of which 1 were waited for; matrix products, arithmetic and copies ran while one was open for 0% of the time, Pallas kernels for 33%

profile of v3, /device:TPU:1, one launch (start us, length us, event | category | flops | bytes accessed | tf_op | source)
XLA Modules:
  0.0 90.1 jit_solution(15641768095568233965)
XLA Ops:
  0.6 2.0 %request_part.1 = (f32[128,128]{1,0:T(8,128)}, f32[536,128]{1,0:T(8,128)}) custom-call(f32[6]{0:T(128)} %theta.1, f32[4,16]{1,0:T(4,128)} %coarse_coords.1, s32[1,384]{1,0:T(1,128)} %coarse.1, f32[4,128]{1,0:T(4,128)} %coords.1, f32[512,128]{1,0:T(8,128)} %values.1, s32[1,128]{1,0:T(1,128)} %fine.1), custom_call_target="tpu_custom_call" | custom-call | tf_op jit(solution)/shard_map/request_part/pallas_call | solution.py:383
  2.6 2.1 %collective-permute-start.1 = (f32[536,128]{1,0:T(8,128)}, f32[536,128]{1,0:T(8,128)S(1)}, u32[]{:S(2)}, u32[]{:S(2)}) collective-permute-start(f32[536,128]{1,0:T(8,128)} %get-tuple-element.7.tile), channel_id=1, source_target_pairs={{15,0},{0,1},{1,2},{2,3},{3,4},{4,5},{5,6},{6,7},{7,8},{8,9},{9,10... | collective-permute-start | bytes 823304 | tf_op jit(solution)/shard_map/ppermute | solution.py:38
  4.8 4.0 %collective-permute-start = (f32[536,128]{1,0:T(8,128)}, f32[536,128]{1,0:T(8,128)S(1)}, u32[]{:S(2)}, u32[]{:S(2)}) collective-permute-start(f32[536,128]{1,0:T(8,128)} %get-tuple-element.7.tile), channel_id=1, source_target_pairs={{0,16},{16,32},{32,48},{48,64},{64,80},{80,96},{96,112},{1,17},{17... | collective-permute-start | bytes 823304 | tf_op jit(solution)/shard_map/ppermute | solution.py:32
  8.7 9.5 %all-to-all-start = ((f32[128,1,128]{2,1,0:T(1,128)}), f32[128,1,128]{2,1,0:T(1,128)S(1)}, u32[]{:S(2)}, u32[]{:S(2)}) async-start(f32[128,1,128]{2,1,0:T(1,128)} %bitcast.17), calls=%async_computation | async-start | bytes 131072 | tf_op jit(solution)/shard_map/all_to_all | solution.py:393
  18.2 0.0 copy-start.2
  18.3 0.0 collective-permute-done.1.left
  18.3 0.0 collective-permute-done.up
  18.3 0.0 copy-start.3
  18.3 0.9 %copy-done.3 = f32[536,128]{1,0:T(8,128)S(1)} copy-done((f32[536,128]{1,0:T(8,128)S(1)}, f32[536,128]{1,0:T(8,128)}, u32[]{:S(2)}) %copy-start.3) | copy-done | bytes 274456
  19.2 3.4 %fine_part.1.after.given = f32[264,640]{1,0:T(8,128)S(1)} custom-call(f32[536,128]{1,0:T(8,128)S(1)} %copy-done.3, f32[536,128]{1,0:T(8,128)S(1)} %collective-permute-done.up, f32[536,128]{1,0:T(8,128)S(1)} %collective-permute-done.1.left), custom_call_target="tpu_custom_call" | custom-call | flops 4000000000 | bytes 1048576 | tf_op jit(solution)/shard_map/fine_part/pallas_call | solution.py:394
  22.6 5.3 %all-to-all-done = f32[128,1,128]{2,1,0:T(1,128)S(1)} async-done(((f32[128,1,128]{2,1,0:T(1,128)}), f32[128,1,128]{2,1,0:T(1,128)S(1)}, u32[]{:S(2)}, u32[]{:S(2)}) %all-to-all-start) | async-done | bytes 65568 | tf_op jit(solution)/shard_map/all_to_all | solution.py:393
  28.0 0.0 copy-done.2
  28.0 1.7 %send_part.1 = f32[3072,128]{1,0:T(8,128)} custom-call(f32[128,128]{1,0:T(8,128)S(1)} %bitcast.12, f32[16,512]{1,0:T(8,128)S(1)} %bitcast.16, f32[264,640]{1,0:T(8,128)S(1)} %fine_part.1.after.given), custom_call_target="tpu_custom_call" | custom-call | tf_op jit(solution)/shard_map/send_part/pallas_call | solution.py:403
  29.6 4.4 %all-to-all-start.1 = ((f32[128,24,128]{2,1,0:T(8,128)}), f32[128,24,128]{2,1,0:T(8,128)S(1)}, u32[]{:S(2)}, u32[]{:S(2)}) async-start(f32[128,24,128]{2,1,0:T(8,128)} %bitcast.4), calls=%async_computation.1 | async-start | bytes 3145728 | tf_op jit(solution)/shard_map/all_to_all | solution.py:411
  34.1 26.1 %fisher_part.1.parts = f32[1312,640]{1,0:T(8,128)S(1)} custom-call(f32[128,128]{1,0:T(8,128)S(1)} %bitcast.13, f32[264,640]{1,0:T(8,128)S(1)} %fine_part.1.after.given), custom_call_target="tpu_custom_call" | custom-call | flops 30000001024 | bytes 1048576 | tf_op jit(solution)/shard_map/fisher_part/pallas_call | solution.py:412
  60.2 0.0 copy-start
  60.2 1.7 %copy-done = f32[1312,640]{1,0:T(8,128)} copy-done((f32[1312,640]{1,0:T(8,128)}, f32[1312,640]{1,0:T(8,128)S(1)}, u32[]{:S(2)}) %copy-start) | copy-done | bytes 3358744
  61.9 0.0 all-to-all-done.1
  61.9 0.0 copy-start.1
  61.9 1.9 %copy-done.1 = f32[1312,640]{1,0:T(8,128)S(1)} copy-done((f32[1312,640]{1,0:T(8,128)S(1)}, f32[1312,640]{1,0:T(8,128)}, u32[]{:S(2)}) %copy-start.1) | copy-done | bytes 3358744
  63.8 5.6 %gradient_part.1 = (f32[512,128]{1,0:T(8,128)}, f32[128,128]{1,0:T(8,128)S(1)}) custom-call(f32[3072,128]{1,0:T(8,128)S(1)} %bitcast.11, f32[1312,640]{1,0:T(8,128)S(1)} %copy-done.1), custom_call_target="tpu_custom_call" | custom-call | tf_op jit(solution)/shard_map/gradient_part/pallas_call | solution.py:432
  69.4 19.3 %all_to_all.33 = f32[128,1,128]{2,1,0:T(1,128)S(1)} all-to-all(f32[128,1,128]{2,1,0:T(1,128)S(1)} %bitcast.15), channel_id=1, replica_groups=mesh['row'=8,'col'=16] {'row','col'}, dimensions={0} | all-to-all | bytes 131072 | tf_op jit(solution)/shard_map/all_to_all | solution.py:445
  88.8 1.4 %solve_part.1 = f32[6]{0:T(128)} custom-call(f32[128,128]{1,0:T(8,128)S(1)} %bitcast.14), custom_call_target="tpu_custom_call" | custom-call | tf_op jit(solution)/shard_map/solve_part/pallas_call | solution.py:446
Async XLA Ops:
  2.6 15.6 %collective-permute-start.1 = (f32[536,128]{1,0:T(8,128)}, f32[536,128]{1,0:T(8,128)S(1)}, u32[]{:S(2)}, u32[]{:S(2)}) collective-permute-start(f32[536,128]{1,0:T(8,128)} %get-tuple-element.7.tile), channel_id=1, source_target_pairs={{15,0},{0,1},{1,2},{2,3},{3,4},{4,5},{5,6},{6,7},{7,8},{8,9},{9,10... | collective-permute-start | bytes 823304 | tf_op jit(solution)/shard_map/ppermute | solution.py:38
  4.8 13.5 %collective-permute-start = (f32[536,128]{1,0:T(8,128)}, f32[536,128]{1,0:T(8,128)S(1)}, u32[]{:S(2)}, u32[]{:S(2)}) collective-permute-start(f32[536,128]{1,0:T(8,128)} %get-tuple-element.7.tile), channel_id=1, source_target_pairs={{0,16},{16,32},{32,48},{48,64},{64,80},{80,96},{96,112},{1,17},{17... | collective-permute-start | bytes 823304 | tf_op jit(solution)/shard_map/ppermute | solution.py:32
  8.7 19.2 %all-to-all-start = ((f32[128,1,128]{2,1,0:T(1,128)}), f32[128,1,128]{2,1,0:T(1,128)S(1)}, u32[]{:S(2)}, u32[]{:S(2)}) async-start(f32[128,1,128]{2,1,0:T(1,128)} %bitcast.17), calls=%async_computation | async-start | bytes 131072 | tf_op jit(solution)/shard_map/all_to_all | solution.py:393
  18.2 9.7 %copy-start.2 = (f32[512,16]{0,1:T(8,128)S(1)}, f32[512,16]{0,1:T(8,128)}, u32[]{:S(2)}) copy-start(f32[512,16]{0,1:T(8,128)} %param.10) | copy-start | bytes 98308
  18.3 1.0 %copy-start.3 = (f32[536,128]{1,0:T(8,128)S(1)}, f32[536,128]{1,0:T(8,128)}, u32[]{:S(2)}) copy-start(f32[536,128]{1,0:T(8,128)} %get-tuple-element.7.tile) | copy-start | bytes 823300
  29.6 32.2 %all-to-all-start.1 = ((f32[128,24,128]{2,1,0:T(8,128)}), f32[128,24,128]{2,1,0:T(8,128)S(1)}, u32[]{:S(2)}, u32[]{:S(2)}) async-start(f32[128,24,128]{2,1,0:T(8,128)} %bitcast.4), calls=%async_computation.1 | async-start | bytes 3145728 | tf_op jit(solution)/shard_map/all_to_all | solution.py:411
  60.2 1.7 %copy-start = (f32[1312,640]{1,0:T(8,128)}, f32[1312,640]{1,0:T(8,128)S(1)}, u32[]{:S(2)}) copy-start(f32[1312,640]{1,0:T(8,128)S(1)} %fisher_part.1.parts) | copy-start | bytes 10076164
  61.9 2.0 %copy-start.1 = (f32[1312,640]{1,0:T(8,128)S(1)}, f32[1312,640]{1,0:T(8,128)}, u32[]{:S(2)}) copy-start(f32[1312,640]{1,0:T(8,128)} %copy-done) | copy-start | bytes 10076164

commit v4 on v3

--- a/solution.py
+++ b/solution.py
@@ -103,40 +103,50 @@
     ahead = [wide(s[0], j) for j in range(8)]
     for g in range(tiles):
         k0 = 8 * g
-        live = range(g, tiles)
-        cols = [{v: wide(s[v], k0 + j) for v in range(g + 1, tiles)} for j in range(8)]
-        for j in range(8):
-            cols[j][g] = ahead[j]
-        if g + 1 < tiles:
+        more = g + 1 < tiles
+        cols = ahead
+        inside = (lane >= k0) & (lane < k0 + 8)
+        mine = jnp.where(inside, (lane == sub + k0).astype(F32), s[g])
+        if more:
+            near = [wide(s[g + 1], k0 + j) for j in range(8)]
             ahead = [wide(s[g + 1], k0 + 8 + j) for j in range(8)]
-        inside = (lane >= k0) & (lane < k0 + 8)
-        s[g] = jnp.where(inside, (lane == sub + k0).astype(F32), s[g])
-        for v in range(g + 1, tiles):
-            s[v] = jnp.where(inside, 0.0, s[v])
+            after = jnp.where(inside, 0.0, s[g + 1])
         pivots = jnp.ones((8, B), F32)
-        pivot = tall(cols[0][g], 0)
+        pivot = tall(cols[0], 0)
+        scaled, rows = [], []
         for k in range(8):
-            col = cols[k]
             pivots = jnp.where(sub == k, pivot, pivots)
             over = 1.0 / pivot
+            at = [tall(cols[k], later) for later in range(k + 1, 8)]
             if k < 7:
-                below = tall(col[g], k + 1)
-                pivot = tall(cols[k + 1][g], k + 1) - (below * below) * over
-            factor = {v: col[v] * over for v in live}
-            factor[g] = jnp.where(sub > k, factor[g], 0.0)
+                pivot = tall(cols[k + 1], k + 1) - (at[0] * at[0]) * over
+            at = [entry * over for entry in at]
+            row = tall(mine, k) * over
+            column = jnp.where(sub > k, cols[k], 0.0)
             for later in range(k + 1, 8):
-                at = tall(col[g], later)
-                for v in live:
-                    cols[later][v] = cols[later][v] - factor[v] * at
-            if g + 1 < tiles:
+                cols[later] = cols[later] - column * at[later - k - 1]
+            mine = mine - column * row
+            scaled.append(at)
+            rows.append(row)
+            if more:
+                for later in range(k + 1, 8):
+                    near[later] = near[later] - near[k] * at[later - k - 1]
                 for j in range(8):
-                    ahead[j] = ahead[j] - factor[g + 1] * tall(col[g + 1], j)
-            row = tall(s[g], k)
-            for v in live:
-                s[v] = s[v] - factor[v] * row
+                    ahead[j] = ahead[j] - near[k] * (tall(near[k], j) * over)
+                after = after - near[k] * row
+        if more:
+            s[g + 1] = after
+        for v in range(g + 2, tiles):
+            col = [wide(s[v], k0 + j) for j in range(8)]
+            x = jnp.where(inside, 0.0, s[v])
+            for k in range(8):
+                for later in range(k + 1, 8):
+                    col[later] = col[later] - col[k] * scaled[k][later - k - 1]
+                x = x - col[k] * rows[k]
+            s[v] = x
         root = lax.rsqrt(pivots)
         root = root * (1.5 - 0.5 * pivots * root * root)
-        out.append(jnp.where(lane <= sub + k0, s[g] * root, 0.0))
+        out.append(jnp.where(lane <= sub + k0, mine * root, 0.0))
     return out
 
 
@@ -312,14 +322,7 @@
     return nt(one_hot, high, None) + nt(one_hot, low, None)
 
 
-def second_kernel(arrived, parts, white_ref, row_ref, v_ref, given, sems):
-    pieces = ((FIELDS, FIELDS + COARSE), (MROW, FIELDS), (0, MROW))
-    copies = [
-        pltpu.make_async_copy(parts.at[first:end], given.at[first:end], sems.at[n]) for n, (first, end) in enumerate(pieces)
-    ]
-    for copy in copies:
-        copy.start()
-    copies[0].wait()
+def second_kernel(arrived, given, white_ref, row_ref, v_ref):
     reps = white_ref.shape[0]
     chunks = reps // B
     held = arrived.shape[0] // chunks
@@ -329,12 +332,10 @@
     for c in range(chunks):
         high, low = halves(arrived[pl.ds(c, held, stride=chunks), :])
         v_ref[B:LEAD, c * B : (c + 1) * B] = nn(hot, high, None) + nn(hot, low, None)
-    copies[1].wait()
     white = nn(given[MROW : MROW + B, :], v_ref[...])
     white_ref[...] = white.T
     cross = nt(white, v_ref[:LEAD, :])
     square = nt(white, white)
-    copies[2].wait()
     part = given[PROW:FIELDS, :B]
     lines = []
     for i in range(6):
@@ -432,13 +433,9 @@
     white, row = pl.pallas_call(
         second_kernel,
         out_shape=(shape(reps, B), shape(devices, B)),
-        in_specs=[vmem, pl.BlockSpec(memory_space=pl.ANY)],
+        in_specs=[vmem] * 2,
         out_specs=(vmem,) * 2,
-        scratch_shapes=[
-            pltpu.VMEM((N, reps), F32),
-            pltpu.VMEM((FIELDS + COARSE, N), F32),
-            pltpu.SemaphoreType.DMA((3,)),
-        ],
+        scratch_shapes=[pltpu.VMEM((N, reps), F32)],
         compiler_params=room(24),
         name="gradient_part",
     )(arrived, parts)

time: 90.4 us -> 88.1 us (0.975)
  Pallas kernels: 40.1 us -> 37.7 us
    pallas_call x1, Pallas kernels: 5.59 us -> 4.13 us  [body(): pl.pallas_call(second_kernel, out_shape=(shape(reps, B), shape(devices, B...]
    pallas_call x1, Pallas kernels: 26.1 us -> 25 us  [body(): pl.pallas_call(first_kernel, out_shape=shape(FIELDS + COARSE, N), in_spec...]
where the time goes in v4:
time: 88.1 us; the launch traced here: 87.8 us
  Pallas kernels  37.7 us (43%)
  starting transfers between devices  20.2 us (23%)
  blocking collectives  19.4 us (22%)
  waiting for transfers between devices  5.19 us (6%)
  local copies, waits for them, and re-layouts  4.6 us (5%)
    pallas_call x1, Pallas kernels, body(): pl.pallas_call(first_kernel, out_shape=shape(FIELDS + COARSE, N), in_spec...  25 us
    all_to_all x1, blocking collectives, body(): rows = lax.all_to_all(row, AXES, 0, 0, tiled=True)  19.4 us
    all_to_all x1, starting transfers between devices, body(): table = lax.all_to_all(request, AXES, 0, 0, tiled=True)  9.52 us
    all_to_all x1, waiting for transfers between devices, body(): table = lax.all_to_all(request, AXES, 0, 0, tiled=True)  5.18 us
    all_to_all x1, starting transfers between devices, body(): arrived = lax.all_to_all(send, AXES, 0, 0, tiled=True)  4.6 us
    unnamed x8, local copies, waits for them, and re-layouts  4.6 us
    pallas_call x1, Pallas kernels, body(): pl.pallas_call(second_kernel, out_shape=(shape(reps, B), shape(devices, B...  4.13 us
    ppermute x1, starting transfers between devices, shifted(): lax.ppermute(value, axis, [(source, source + steps) for source in range(f...  3.95 us
  transfers between devices with their start and end apart: 4, of which 1 were waited for; matrix products, arithmetic and copies ran while one was open for 0% of the time, Pallas kernels for 33%

profile of v4, /device:TPU:1, one launch (start us, length us, event | category | flops | bytes accessed | tf_op | source)
XLA Modules:
  0.0 87.8 jit_solution(13017140466944930756)
XLA Ops:
  0.6 2.0 %request_part.1 = (f32[128,128]{1,0:T(8,128)}, f32[536,128]{1,0:T(8,128)}) custom-call(f32[6]{0:T(128)} %theta.1, f32[4,16]{1,0:T(4,128)} %coarse_coords.1, s32[1,384]{1,0:T(1,128)} %coarse.1, f32[4,128]{1,0:T(4,128)} %coords.1, f32[512,128]{1,0:T(8,128)} %values.1, s32[1,128]{1,0:T(1,128)} %fine.1), custom_call_target="tpu_custom_call" | custom-call | tf_op jit(solution)/shard_map/request_part/pallas_call | solution.py:384
  2.6 2.1 %collective-permute-start.1 = (f32[536,128]{1,0:T(8,128)}, f32[536,128]{1,0:T(8,128)S(1)}, u32[]{:S(2)}, u32[]{:S(2)}) collective-permute-start(f32[536,128]{1,0:T(8,128)} %get-tuple-element.7.tile), channel_id=1, source_target_pairs={{15,0},{0,1},{1,2},{2,3},{3,4},{4,5},{5,6},{6,7},{7,8},{8,9},{9,10... | collective-permute-start | bytes 823304 | tf_op jit(solution)/shard_map/ppermute | solution.py:38
  4.8 4.0 %collective-permute-start = (f32[536,128]{1,0:T(8,128)}, f32[536,128]{1,0:T(8,128)S(1)}, u32[]{:S(2)}, u32[]{:S(2)}) collective-permute-start(f32[536,128]{1,0:T(8,128)} %get-tuple-element.7.tile), channel_id=1, source_target_pairs={{0,16},{16,32},{32,48},{48,64},{64,80},{80,96},{96,112},{1,17},{17... | collective-permute-start | bytes 823304 | tf_op jit(solution)/shard_map/ppermute | solution.py:32
  8.7 9.5 %all-to-all-start = ((f32[128,1,128]{2,1,0:T(1,128)}), f32[128,1,128]{2,1,0:T(1,128)S(1)}, u32[]{:S(2)}, u32[]{:S(2)}) async-start(f32[128,1,128]{2,1,0:T(1,128)} %bitcast.17), calls=%async_computation | async-start | bytes 131072 | tf_op jit(solution)/shard_map/all_to_all | solution.py:394
  18.2 0.0 copy-start.2
  18.3 0.0 collective-permute-done.1.left
  18.3 0.0 collective-permute-done.up
  18.3 0.0 copy-start.3
  18.3 0.9 %copy-done.3 = f32[536,128]{1,0:T(8,128)S(1)} copy-done((f32[536,128]{1,0:T(8,128)S(1)}, f32[536,128]{1,0:T(8,128)}, u32[]{:S(2)}) %copy-start.3) | copy-done | bytes 274456
  19.2 3.5 %fine_part.1.after.given = f32[264,640]{1,0:T(8,128)S(1)} custom-call(f32[536,128]{1,0:T(8,128)S(1)} %copy-done.3, f32[536,128]{1,0:T(8,128)S(1)} %collective-permute-done.up, f32[536,128]{1,0:T(8,128)S(1)} %collective-permute-done.1.left), custom_call_target="tpu_custom_call" | custom-call | flops 4000000000 | bytes 1048576 | tf_op jit(solution)/shard_map/fine_part/pallas_call | solution.py:395
  22.8 5.2 %all-to-all-done = f32[128,1,128]{2,1,0:T(1,128)S(1)} async-done(((f32[128,1,128]{2,1,0:T(1,128)}), f32[128,1,128]{2,1,0:T(1,128)S(1)}, u32[]{:S(2)}, u32[]{:S(2)}) %all-to-all-start) | async-done | bytes 65568 | tf_op jit(solution)/shard_map/all_to_all | solution.py:394
  28.0 0.0 copy-done.2
  28.0 1.7 %send_part.1 = f32[3072,128]{1,0:T(8,128)} custom-call(f32[128,128]{1,0:T(8,128)S(1)} %bitcast.12, f32[16,512]{1,0:T(8,128)S(1)} %bitcast.16, f32[264,640]{1,0:T(8,128)S(1)} %fine_part.1.after.given), custom_call_target="tpu_custom_call" | custom-call | tf_op jit(solution)/shard_map/send_part/pallas_call | solution.py:404
  29.6 4.6 %all-to-all-start.1 = ((f32[128,24,128]{2,1,0:T(8,128)}), f32[128,24,128]{2,1,0:T(8,128)S(1)}, u32[]{:S(2)}, u32[]{:S(2)}) async-start(f32[128,24,128]{2,1,0:T(8,128)} %bitcast.4), calls=%async_computation.1 | async-start | bytes 3145728 | tf_op jit(solution)/shard_map/all_to_all | solution.py:412
  34.3 25.0 %fisher_part.1.given = f32[1312,640]{1,0:T(8,128)S(1)} custom-call(f32[128,128]{1,0:T(8,128)S(1)} %bitcast.13, f32[264,640]{1,0:T(8,128)S(1)} %fine_part.1.after.given), custom_call_target="tpu_custom_call" | custom-call | flops 30000001024 | bytes 1048576 | tf_op jit(solution)/shard_map/fisher_part/pallas_call | solution.py:413
  59.3 0.0 copy-start
  59.3 1.7 %copy-done = f32[1312,640]{1,0:T(8,128)} copy-done((f32[1312,640]{1,0:T(8,128)}, f32[1312,640]{1,0:T(8,128)S(1)}, u32[]{:S(2)}) %copy-start) | copy-done | bytes 3358744
  61.0 0.0 all-to-all-done.1
  61.0 0.0 copy-start.1
  61.0 1.9 %copy-done.1 = f32[1312,640]{1,0:T(8,128)S(1)} copy-done((f32[1312,640]{1,0:T(8,128)S(1)}, f32[1312,640]{1,0:T(8,128)}, u32[]{:S(2)}) %copy-start.1) | copy-done | bytes 3358744
  62.9 4.1 %gradient_part.1 = (f32[512,128]{1,0:T(8,128)}, f32[128,128]{1,0:T(8,128)S(1)}) custom-call(f32[3072,128]{1,0:T(8,128)S(1)} %bitcast.11, f32[1312,640]{1,0:T(8,128)S(1)} %copy-done.1), custom_call_target="tpu_custom_call" | custom-call | tf_op jit(solution)/shard_map/gradient_part/pallas_call | solution.py:433
  67.1 19.4 %all_to_all.33 = f32[128,1,128]{2,1,0:T(1,128)S(1)} all-to-all(f32[128,1,128]{2,1,0:T(1,128)S(1)} %bitcast.15), channel_id=1, replica_groups=mesh['row'=8,'col'=16] {'row','col'}, dimensions={0} | all-to-all | bytes 131072 | tf_op jit(solution)/shard_map/all_to_all | solution.py:442
  86.4 1.4 %solve_part.1 = f32[6]{0:T(128)} custom-call(f32[128,128]{1,0:T(8,128)S(1)} %bitcast.14), custom_call_target="tpu_custom_call" | custom-call | tf_op jit(solution)/shard_map/solve_part/pallas_call | solution.py:443
Async XLA Ops:
  2.6 15.6 %collective-permute-start.1 = (f32[536,128]{1,0:T(8,128)}, f32[536,128]{1,0:T(8,128)S(1)}, u32[]{:S(2)}, u32[]{:S(2)}) collective-permute-start(f32[536,128]{1,0:T(8,128)} %get-tuple-element.7.tile), channel_id=1, source_target_pairs={{15,0},{0,1},{1,2},{2,3},{3,4},{4,5},{5,6},{6,7},{7,8},{8,9},{9,10... | collective-permute-start | bytes 823304 | tf_op jit(solution)/shard_map/ppermute | solution.py:38
  4.8 13.5 %collective-permute-start = (f32[536,128]{1,0:T(8,128)}, f32[536,128]{1,0:T(8,128)S(1)}, u32[]{:S(2)}, u32[]{:S(2)}) collective-permute-start(f32[536,128]{1,0:T(8,128)} %get-tuple-element.7.tile), channel_id=1, source_target_pairs={{0,16},{16,32},{32,48},{48,64},{64,80},{80,96},{96,112},{1,17},{17... | collective-permute-start | bytes 823304 | tf_op jit(solution)/shard_map/ppermute | solution.py:32
  8.7 19.2 %all-to-all-start = ((f32[128,1,128]{2,1,0:T(1,128)}), f32[128,1,128]{2,1,0:T(1,128)S(1)}, u32[]{:S(2)}, u32[]{:S(2)}) async-start(f32[128,1,128]{2,1,0:T(1,128)} %bitcast.17), calls=%async_computation | async-start | bytes 131072 | tf_op jit(solution)/shard_map/all_to_all | solution.py:394
  18.2 9.7 %copy-start.2 = (f32[512,16]{0,1:T(8,128)S(1)}, f32[512,16]{0,1:T(8,128)}, u32[]{:S(2)}) copy-start(f32[512,16]{0,1:T(8,128)} %param.10) | copy-start | bytes 98308
  18.3 1.0 %copy-start.3 = (f32[536,128]{1,0:T(8,128)S(1)}, f32[536,128]{1,0:T(8,128)}, u32[]{:S(2)}) copy-start(f32[536,128]{1,0:T(8,128)} %get-tuple-element.7.tile) | copy-start | bytes 823300
  29.6 31.4 %all-to-all-start.1 = ((f32[128,24,128]{2,1,0:T(8,128)}), f32[128,24,128]{2,1,0:T(8,128)S(1)}, u32[]{:S(2)}, u32[]{:S(2)}) async-start(f32[128,24,128]{2,1,0:T(8,128)} %bitcast.4), calls=%async_computation.1 | async-start | bytes 3145728 | tf_op jit(solution)/shard_map/all_to_all | solution.py:412
  59.3 1.7 %copy-start = (f32[1312,640]{1,0:T(8,128)}, f32[1312,640]{1,0:T(8,128)S(1)}, u32[]{:S(2)}) copy-start(f32[1312,640]{1,0:T(8,128)S(1)} %fisher_part.1.given) | copy-start | bytes 10076164
  61.0 2.0 %copy-start.1 = (f32[1312,640]{1,0:T(8,128)S(1)}, f32[1312,640]{1,0:T(8,128)}, u32[]{:S(2)}) copy-start(f32[1312,640]{1,0:T(8,128)} %copy-done) | copy-start | bytes 10076164

commit v5 on v4

--- a/solution.py
+++ b/solution.py
@@ -23,7 +23,7 @@
 CP = 16
 MOST = 6
 FINE, PLACE, WANTED, SPREAD, VARIANCE, NUG, TAIL = 4, 5, 8, 11, 15, 16, 24
-MROW, PROW, FIELDS = 768, 896, 928
+MROW, PROW, TOTAL_ROWS = 640, 768, 776
 
 
 def shifted(value, axis, steps):
@@ -241,12 +241,10 @@
     down = jnp.concatenate(across + [live] + [jnp.zeros((B - 5, N), F32)], axis=0).T
     variance = jnp.concatenate([ends[6:7], ends[6:7, : N - COARSE]], axis=1)
     nugget = jnp.concatenate([ends[7:8], ends[7:8, : N - COARSE]], axis=1)
-    out_ref[FIELDS : FIELDS + 2 * B, :LEAD] = given[: 2 * B, :LEAD]
-    out_ref[FIELDS:, LEAD:] = jnp.broadcast_to(ends[0:1], (B, COARSE)).T
     for r in range(N // B):
         here = slice(r * B, (r + 1) * B)
         kernel, common, squares = pair(down[here], across, variance, down[here, 4:5], live)
-        for i, part in enumerate([kernel] + [common * square for square in squares]):
+        for i, part in enumerate([common * square for square in squares]):
             there = slice(i * N, (i + 1) * N)
             f_ref[here, there], f_ref[N + r * B : N + (r + 1) * B, there], f3_ref[here, there] = thirds(part)
         same = iota((B, N), 0) + r * B == iota((B, N), 1)
@@ -290,10 +288,10 @@
     twice = jnp.concatenate([jnp.concatenate([part, part], axis=1) for part in parts], axis=0)
     large = nn(twice, f_ref[...], None)
     small = large[B:] + nn(parts[0], f3_ref[...], None)
-    for i in range(5):
+    y_ref[:B, :] = m * (live * nugget)
+    for i in range(4):
         there = slice(i * N, (i + 1) * N)
-        y_ref[i * B : (i + 1) * B, :] = large[:B, there] + small[:, there]
-    y_ref[5 * B :, :] = m * (live * nugget)
+        y_ref[(i + 1) * B : (i + 2) * B, :] = large[:B, there] + small[:, there]
     high, low = halves(y_ref[...])
     out_ref[:MROW, :LEAD] = -three_terms((high[:, :LEAD], low[:, :LEAD]), halves(k_ref[:LEAD, :LEAD]), nn)
     out_ref[:MROW, LEAD:] = three_terms((high, low), parts, nt)
@@ -305,16 +303,29 @@
             total = total + x[:, c * B : (c + 1) * B]
         return total
 
-    sums = []
-    for i in range(6):
+    def z_of(i):
+        return out_ref[i * B : (i + 1) * B, :LEAD]
+
+    def g_of(i):
+        return out_ref[i * B : (i + 1) * B, LEAD:]
+
+    def line(x):
+        return jnp.sum(x, axis=0, keepdims=True)
+
+    eye = (iota((B, B), 0) == iota((B, B), 1)).astype(F32)
+    pairs, traces = {}, [line(folded(g_of(i) * eye)) for i in range(5)]
+    for i in range(5):
         for j in range(i + 1):
-            lead_part = out_ref[i * B : (i + 1) * B, :LEAD] * y_ref[j * B : (j + 1) * B, :LEAD]
-            own_part = out_ref[i * B : (i + 1) * B, LEAD:] * out_ref[j * B : (j + 1) * B, LEAD:]
-            sums.append(jnp.sum(2.0 * folded(lead_part) + folded(own_part), axis=0, keepdims=True))
-    for i in range(6):
-        sums.append(jnp.sum(folded(y_ref[i * B : (i + 1) * B, :] * m), axis=0, keepdims=True))
-    sums.append(jnp.zeros((5, B), F32))
-    out_ref[PROW:FIELDS, :B] = jnp.concatenate(sums, axis=0)
+            lead_part = z_of(i) * y_ref[j * B : (j + 1) * B, :LEAD]
+            pairs[i, j] = line(2.0 * folded(lead_part) + folded(g_of(i) * g_of(j)))
+    ones = jnp.ones((1, B), F32)
+    sums = [pairs[0, 0] + (ones - 2.0 * traces[0])]
+    for i in range(1, 5):
+        sums += [traces[i] - pairs[i, 0]] + [pairs[i, j] for j in range(1, i + 1)]
+    sums += [traces[0] - pairs[0, 0]] + [pairs[j, 0] for j in range(1, 5)] + [pairs[0, 0]]
+    sums += [ones - traces[0]] + traces[1:] + [traces[0]]
+    sums.append(jnp.zeros((B - 27, B), F32))
+    out_ref[PROW:, :B] = jnp.broadcast_to(line(jnp.concatenate(sums, axis=0).T), (8, B))
 
 
 def picked2(one_hot, table):
@@ -322,13 +333,14 @@
     return nt(one_hot, high, None) + nt(one_hot, low, None)
 
 
-def second_kernel(arrived, given, white_ref, row_ref, v_ref):
+def second_kernel(arrived, given, fine, white_ref, row_ref, v_ref):
     reps = white_ref.shape[0]
     chunks = reps // B
     held = arrived.shape[0] // chunks
-    v_ref[:B, :] = given[FIELDS : FIELDS + B, :reps]
-    v_ref[LEAD:, :] = given[FIELDS + B : FIELDS + 2 * B, :reps]
-    hot = (given[FIELDS:, LEAD : LEAD + 1] == iota((COARSE, held), 1).astype(F32)).astype(BF16)
+    v_ref[:B, :] = fine[:B, :reps]
+    v_ref[LEAD:, :] = fine[B : 2 * B, :reps]
+    place = jnp.broadcast_to(fine[2 * B : 2 * B + 1, 2 * B :], (B, COARSE)).T[:, :1]
+    hot = (place == iota((COARSE, held), 1).astype(F32)).astype(BF16)
     for c in range(chunks):
         high, low = halves(arrived[pl.ds(c, held, stride=chunks), :])
         v_ref[B:LEAD, c * B : (c + 1) * B] = nn(hot, high, None) + nn(hot, low, None)
@@ -336,15 +348,18 @@
     white_ref[...] = white.T
     cross = nt(white, v_ref[:LEAD, :])
     square = nt(white, white)
-    part = given[PROW:FIELDS, :B]
-    lines = []
-    for i in range(6):
+    eye = (iota((B, B), 0) == iota((B, B), 1)).astype(F32)
+    leads, owns = [], []
+    for i in range(5):
         both = given[i * B : (i + 1) * B, :LEAD] * cross
-        both = (both[:, :B] + both[:, B : 2 * B]) + (both[:, 2 * B : 3 * B] + both[:, 3 * B :])
-        both = both + 0.5 * (given[i * B : (i + 1) * B, LEAD:] * square)
-        lines.append(jnp.sum(both, axis=0, keepdims=True) - (0.5 * reps) * part[21 + i : 22 + i, :])
-    whole = jnp.concatenate([(0.5 * reps) * part[:21, :]] + lines + [jnp.zeros((B - 27, B), F32)], axis=0)
-    row_ref[...] = jnp.broadcast_to(jnp.sum(whole.T, axis=0, keepdims=True), row_ref.shape)
+        leads.append((both[:, :B] + both[:, B : 2 * B]) + (both[:, 2 * B : 3 * B] + both[:, 3 * B :]))
+        owns.append(0.5 * (given[i * B : (i + 1) * B, LEAD:] * square))
+    terms = [0.5 * (eye * square) - owns[0] - leads[0]] + [leads[i] + owns[i] for i in (1, 2, 3, 4, 0)]
+    terms = [jnp.sum(term, axis=0, keepdims=True) for term in terms]
+    whole = jnp.concatenate([jnp.zeros((21, B), F32)] + terms + [jnp.zeros((B - 27, B), F32)], axis=0)
+    weight = jnp.where(iota((1, B), 1) < 21, 0.5 * reps, -0.5 * reps)
+    row = jnp.sum(whole.T, axis=0, keepdims=True) + weight * given[PROW : PROW + 1, :B]
+    row_ref[...] = jnp.broadcast_to(row, row_ref.shape)
 
 
 def third_kernel(rows, step_ref):
@@ -412,7 +427,7 @@
     arrived = lax.all_to_all(send, AXES, 0, 0, tiled=True)
     parts = pl.pallas_call(
         first_kernel,
-        out_shape=shape(FIELDS + COARSE, N),
+        out_shape=shape(TOTAL_ROWS, N),
         in_specs=[vmem] * 2,
         out_specs=vmem,
         scratch_shapes=[
@@ -422,9 +437,9 @@
             pltpu.VMEM((B, N), F32),
             pltpu.VMEM((N, 6 * B), BF16),
             pltpu.VMEM((6 * B, N), BF16),
-            pltpu.VMEM((2 * N, 5 * N), BF16),
-            pltpu.VMEM((N, 5 * N), BF16),
-            pltpu.VMEM((6 * B, N), F32),
+            pltpu.VMEM((2 * N, 4 * N), BF16),
+            pltpu.VMEM((N, 4 * N), BF16),
+            pltpu.VMEM((5 * B, N), F32),
         ],
         compiler_params=room(36),
         cost_estimate=cost(30 * 10**9),
@@ -433,12 +448,12 @@
     white, row = pl.pallas_call(
         second_kernel,
         out_shape=(shape(reps, B), shape(devices, B)),
-        in_specs=[vmem] * 2,
+        in_specs=[vmem] * 3,
         out_specs=(vmem,) * 2,
         scratch_shapes=[pltpu.VMEM((N, reps), F32)],
         compiler_params=room(24),
         name="gradient_part",
-    )(arrived, parts)
+    )(arrived, parts, fine)
     rows = lax.all_to_all(row, AXES, 0, 0, tiled=True)
     step = pl.pallas_call(
         third_kernel,

time: 88.1 us -> 86.2 us (0.978)
  Pallas kernels: 37.7 us -> 36.7 us
    pallas_call x1, Pallas kernels: 25 us -> 23.7 us  [body(): pl.pallas_call(first_kernel, out_shape=shape(TOTAL_ROWS, N), in_specs=[vm...]
  transfers between devices with their start and end apart: 4 -> 4, of which waited for: 1 -> 1; matrix products, arithmetic and copies ran while one was open for 0% -> 0% of each run, Pallas kernels for 33% -> 32%
where the time goes in v5:
time: 86.2 us; the launch traced here: 85.9 us
  Pallas kernels  36.7 us (43%)
  starting transfers between devices  20.2 us (23%)
  blocking collectives  19.3 us (22%)
  waiting for transfers between devices  5.19 us (6%)
  local copies, waits for them, and re-layouts  3.8 us (4%)
    pallas_call x1, Pallas kernels, body(): pl.pallas_call(first_kernel, out_shape=shape(TOTAL_ROWS, N), in_specs=[vm...  23.7 us
    all_to_all x1, blocking collectives, body(): rows = lax.all_to_all(row, AXES, 0, 0, tiled=True)  19.3 us
    all_to_all x1, starting transfers between devices, body(): table = lax.all_to_all(request, AXES, 0, 0, tiled=True)  9.52 us
    all_to_all x1, waiting for transfers between devices, body(): table = lax.all_to_all(request, AXES, 0, 0, tiled=True)  5.18 us
    all_to_all x1, starting transfers between devices, body(): arrived = lax.all_to_all(send, AXES, 0, 0, tiled=True)  4.6 us
    pallas_call x1, Pallas kernels, body(): pl.pallas_call(second_kernel, out_shape=(shape(reps, B), shape(devices, B...  4.37 us
    ppermute x1, starting transfers between devices, shifted(): lax.ppermute(value, axis, [(source, source + steps) for source in range(f...  3.95 us
    unnamed x8, local copies, waits for them, and re-layouts  3.8 us
  transfers between devices with their start and end apart: 4, of which 1 were waited for; matrix products, arithmetic and copies ran while one was open for 0% of the time, Pallas kernels for 32%

profile of v5, /device:TPU:1, one launch (start us, length us, event | category | flops | bytes accessed | tf_op | source)
XLA Modules:
  0.0 85.9 jit_solution(5227435452688600960)
XLA Ops:
  0.6 2.0 %request_part.1 = (f32[128,128]{1,0:T(8,128)}, f32[536,128]{1,0:T(8,128)}) custom-call(f32[6]{0:T(128)} %theta.1, f32[4,16]{1,0:T(4,128)} %coarse_coords.1, s32[1,384]{1,0:T(1,128)} %coarse.1, f32[4,128]{1,0:T(4,128)} %coords.1, f32[512,128]{1,0:T(8,128)} %values.1, s32[1,128]{1,0:T(1,128)} %fine.1), custom_call_target="tpu_custom_call" | custom-call | tf_op jit(solution)/shard_map/request_part/pallas_call | solution.py:399
  2.6 2.1 %collective-permute-start.1 = (f32[536,128]{1,0:T(8,128)}, f32[536,128]{1,0:T(8,128)S(1)}, u32[]{:S(2)}, u32[]{:S(2)}) collective-permute-start(f32[536,128]{1,0:T(8,128)} %get-tuple-element.7.tile), channel_id=1, source_target_pairs={{15,0},{0,1},{1,2},{2,3},{3,4},{4,5},{5,6},{6,7},{7,8},{8,9},{9,10... | collective-permute-start | bytes 823304 | tf_op jit(solution)/shard_map/ppermute | solution.py:38
  4.8 4.0 %collective-permute-start = (f32[536,128]{1,0:T(8,128)}, f32[536,128]{1,0:T(8,128)S(1)}, u32[]{:S(2)}, u32[]{:S(2)}) collective-permute-start(f32[536,128]{1,0:T(8,128)} %get-tuple-element.7.tile), channel_id=1, source_target_pairs={{0,16},{16,32},{32,48},{48,64},{64,80},{80,96},{96,112},{1,17},{17... | collective-permute-start | bytes 823304 | tf_op jit(solution)/shard_map/ppermute | solution.py:32
  8.7 9.5 %all-to-all-start = ((f32[128,1,128]{2,1,0:T(1,128)}), f32[128,1,128]{2,1,0:T(1,128)S(1)}, u32[]{:S(2)}, u32[]{:S(2)}) async-start(f32[128,1,128]{2,1,0:T(1,128)} %bitcast.17), calls=%async_computation | async-start | bytes 131072 | tf_op jit(solution)/shard_map/all_to_all | solution.py:409
  18.2 0.0 copy-start.2
  18.3 0.0 collective-permute-done.1.left
  18.3 0.0 collective-permute-done.up
  18.3 0.0 copy-start.3
  18.3 0.9 %copy-done.3 = f32[536,128]{1,0:T(8,128)S(1)} copy-done((f32[536,128]{1,0:T(8,128)S(1)}, f32[536,128]{1,0:T(8,128)}, u32[]{:S(2)}) %copy-start.3) | copy-done | bytes 274456
  19.2 3.5 %fine_part.1.after.given.fine = f32[264,640]{1,0:T(8,128)S(1)} custom-call(f32[536,128]{1,0:T(8,128)S(1)} %copy-done.3, f32[536,128]{1,0:T(8,128)S(1)} %collective-permute-done.up, f32[536,128]{1,0:T(8,128)S(1)} %collective-permute-done.1.left), custom_call_target="tpu_custom_call" | custom-call | flops 4000000000 | bytes 1048576 | tf_op jit(solution)/shard_map/fine_part/pallas_call | solution.py:410
  22.8 5.2 %all-to-all-done = f32[128,1,128]{2,1,0:T(1,128)S(1)} async-done(((f32[128,1,128]{2,1,0:T(1,128)}), f32[128,1,128]{2,1,0:T(1,128)S(1)}, u32[]{:S(2)}, u32[]{:S(2)}) %all-to-all-start) | async-done | bytes 65568 | tf_op jit(solution)/shard_map/all_to_all | solution.py:409
  28.0 0.0 copy-done.2
  28.0 1.7 %send_part.1 = f32[3072,128]{1,0:T(8,128)} custom-call(f32[128,128]{1,0:T(8,128)S(1)} %bitcast.12, f32[16,512]{1,0:T(8,128)S(1)} %bitcast.16, f32[264,640]{1,0:T(8,128)S(1)} %fine_part.1.after.given.fine), custom_call_target="tpu_custom_call" | custom-call | tf_op jit(solution)/shard_map/send_part/pallas_call | solution.py:419
  29.6 4.6 %all-to-all-start.1 = ((f32[128,24,128]{2,1,0:T(8,128)}), f32[128,24,128]{2,1,0:T(8,128)S(1)}, u32[]{:S(2)}, u32[]{:S(2)}) async-start(f32[128,24,128]{2,1,0:T(8,128)} %bitcast.4), calls=%async_computation.1 | async-start | bytes 3145728 | tf_op jit(solution)/shard_map/all_to_all | solution.py:427
  34.2 23.7 %fisher_part.1.given = f32[776,640]{1,0:T(8,128)S(1)} custom-call(f32[128,128]{1,0:T(8,128)S(1)} %bitcast.13, f32[264,640]{1,0:T(8,128)S(1)} %fine_part.1.after.given.fine), custom_call_target="tpu_custom_call" | custom-call | flops 30000001024 | bytes 1048576 | tf_op jit(solution)/shard_map/fisher_part/pallas_call | solution.py:428
  58.0 0.0 copy-start
  58.0 1.3 %copy-done = f32[776,640]{1,0:T(8,128)} copy-done((f32[776,640]{1,0:T(8,128)}, f32[776,640]{1,0:T(8,128)S(1)}, u32[]{:S(2)}) %copy-start) | copy-done | bytes 1986584
  59.3 0.0 all-to-all-done.1
  59.3 0.0 copy-start.1
  59.3 1.6 %copy-done.1 = f32[776,640]{1,0:T(8,128)S(1)} copy-done((f32[776,640]{1,0:T(8,128)S(1)}, f32[776,640]{1,0:T(8,128)}, u32[]{:S(2)}) %copy-start.1) | copy-done | bytes 1986584
  60.8 4.4 %gradient_part.1 = (f32[512,128]{1,0:T(8,128)}, f32[128,128]{1,0:T(8,128)S(1)}) custom-call(f32[3072,128]{1,0:T(8,128)S(1)} %bitcast.11, f32[776,640]{1,0:T(8,128)S(1)} %copy-done.1, f32[264,640]{1,0:T(8,128)S(1)} %fine_part.1.after.given.fine), custom_call_target="tpu_custom_call" | custom-call | tf_op jit(solution)/shard_map/gradient_part/pallas_call | solution.py:448
  65.2 19.3 %all_to_all.33 = f32[128,1,128]{2,1,0:T(1,128)S(1)} all-to-all(f32[128,1,128]{2,1,0:T(1,128)S(1)} %bitcast.15), channel_id=1, replica_groups=mesh['row'=8,'col'=16] {'row','col'}, dimensions={0} | all-to-all | bytes 131072 | tf_op jit(solution)/shard_map/all_to_all | solution.py:457
  84.5 1.4 %solve_part.1 = f32[6]{0:T(128)} custom-call(f32[128,128]{1,0:T(8,128)S(1)} %bitcast.14), custom_call_target="tpu_custom_call" | custom-call | tf_op jit(solution)/shard_map/solve_part/pallas_call | solution.py:458
Async XLA Ops:
  2.6 15.6 %collective-permute-start.1 = (f32[536,128]{1,0:T(8,128)}, f32[536,128]{1,0:T(8,128)S(1)}, u32[]{:S(2)}, u32[]{:S(2)}) collective-permute-start(f32[536,128]{1,0:T(8,128)} %get-tuple-element.7.tile), channel_id=1, source_target_pairs={{15,0},{0,1},{1,2},{2,3},{3,4},{4,5},{5,6},{6,7},{7,8},{8,9},{9,10... | collective-permute-start | bytes 823304 | tf_op jit(solution)/shard_map/ppermute | solution.py:38
  4.8 13.5 %collective-permute-start = (f32[536,128]{1,0:T(8,128)}, f32[536,128]{1,0:T(8,128)S(1)}, u32[]{:S(2)}, u32[]{:S(2)}) collective-permute-start(f32[536,128]{1,0:T(8,128)} %get-tuple-element.7.tile), channel_id=1, source_target_pairs={{0,16},{16,32},{32,48},{48,64},{64,80},{80,96},{96,112},{1,17},{17... | collective-permute-start | bytes 823304 | tf_op jit(solution)/shard_map/ppermute | solution.py:32
  8.7 19.2 %all-to-all-start = ((f32[128,1,128]{2,1,0:T(1,128)}), f32[128,1,128]{2,1,0:T(1,128)S(1)}, u32[]{:S(2)}, u32[]{:S(2)}) async-start(f32[128,1,128]{2,1,0:T(1,128)} %bitcast.17), calls=%async_computation | async-start | bytes 131072 | tf_op jit(solution)/shard_map/all_to_all | solution.py:409
  18.2 9.7 %copy-start.2 = (f32[512,16]{0,1:T(8,128)S(1)}, f32[512,16]{0,1:T(8,128)}, u32[]{:S(2)}) copy-start(f32[512,16]{0,1:T(8,128)} %param.10) | copy-start | bytes 98308
  18.3 1.0 %copy-start.3 = (f32[536,128]{1,0:T(8,128)S(1)}, f32[536,128]{1,0:T(8,128)}, u32[]{:S(2)}) copy-start(f32[536,128]{1,0:T(8,128)} %get-tuple-element.7.tile) | copy-start | bytes 823300
  29.6 29.6 %all-to-all-start.1 = ((f32[128,24,128]{2,1,0:T(8,128)}), f32[128,24,128]{2,1,0:T(8,128)S(1)}, u32[]{:S(2)}, u32[]{:S(2)}) async-start(f32[128,24,128]{2,1,0:T(8,128)} %bitcast.4), calls=%async_computation.1 | async-start | bytes 3145728 | tf_op jit(solution)/shard_map/all_to_all | solution.py:427
  58.0 1.3 %copy-start = (f32[776,640]{1,0:T(8,128)}, f32[776,640]{1,0:T(8,128)S(1)}, u32[]{:S(2)}) copy-start(f32[776,640]{1,0:T(8,128)S(1)} %fisher_part.1.given) | copy-start | bytes 5959684
  59.3 1.6 %copy-start.1 = (f32[776,640]{1,0:T(8,128)S(1)}, f32[776,640]{1,0:T(8,128)}, u32[]{:S(2)}) copy-start(f32[776,640]{1,0:T(8,128)} %copy-done) | copy-start | bytes 5959684

commit v6 on v5

--- a/solution.py
+++ b/solution.py
@@ -333,21 +333,26 @@
     return nt(one_hot, high, None) + nt(one_hot, low, None)
 
 
-def second_kernel(arrived, given, fine, white_ref, row_ref, v_ref):
+def second_kernel(arrived, given, fine, white_ref, row_ref, v1_ref, v2_ref):
     reps = white_ref.shape[0]
     chunks = reps // B
     held = arrived.shape[0] // chunks
-    v_ref[:B, :] = fine[:B, :reps]
-    v_ref[LEAD:, :] = fine[B : 2 * B, :reps]
+    v1_ref[:B, :], v2_ref[:B, :] = halves(fine[:B, :reps])
+    v1_ref[LEAD:, :], v2_ref[LEAD:, :] = halves(fine[B : 2 * B, :reps])
     place = jnp.broadcast_to(fine[2 * B : 2 * B + 1, 2 * B :], (B, COARSE)).T[:, :1]
     hot = (place == iota((COARSE, held), 1).astype(F32)).astype(BF16)
     for c in range(chunks):
         high, low = halves(arrived[pl.ds(c, held, stride=chunks), :])
-        v_ref[B:LEAD, c * B : (c + 1) * B] = nn(hot, high, None) + nn(hot, low, None)
-    white = nn(given[MROW : MROW + B, :], v_ref[...])
+        v1_ref[B:LEAD, c * B : (c + 1) * B] = nn(hot, high, None).astype(BF16)
+        v2_ref[B:LEAD, c * B : (c + 1) * B] = nn(hot, low, None).astype(BF16)
+    parts = thirds(given[MROW : MROW + B, :])
+    first = nn(jnp.concatenate(parts, axis=0), v1_ref[...], None)
+    second = nn(jnp.concatenate(parts[:2], axis=0), v2_ref[...], None)
+    white = first[:B] + ((first[B : 2 * B] + second[:B]) + (first[2 * B :] + second[B:]))
     white_ref[...] = white.T
-    cross = nt(white, v_ref[:LEAD, :])
-    square = nt(white, white)
+    split = halves(white)
+    cross = three_terms(split, (v1_ref[:LEAD, :], v2_ref[:LEAD, :]), nt)
+    square = three_terms(split, split, nt)
     eye = (iota((B, B), 0) == iota((B, B), 1)).astype(F32)
     leads, owns = [], []
     for i in range(5):
@@ -450,7 +455,7 @@
         out_shape=(shape(reps, B), shape(devices, B)),
         in_specs=[vmem] * 3,
         out_specs=(vmem,) * 2,
-        scratch_shapes=[pltpu.VMEM((N, reps), F32)],
+        scratch_shapes=[pltpu.VMEM((N, reps), BF16), pltpu.VMEM((N, reps), BF16)],
         compiler_params=room(24),
         name="gradient_part",
     )(arrived, parts, fine)

time: 86.2 us -> 85.5 us (level)
  no operation moved by 1% of the time
where the time goes in v6:
time: 85.5 us; the launch traced here: 85.2 us
  Pallas kernels  36 us (42%)
  starting transfers between devices  20.2 us (24%)
  blocking collectives  19.4 us (23%)
  waiting for transfers between devices  5.19 us (6%)
  local copies, waits for them, and re-layouts  3.8 us (4%)
    pallas_call x1, Pallas kernels, body(): pl.pallas_call(first_kernel, out_shape=shape(TOTAL_ROWS, N), in_specs=[vm...  23.7 us
    all_to_all x1, blocking collectives, body(): rows = lax.all_to_all(row, AXES, 0, 0, tiled=True)  19.4 us
    all_to_all x1, starting transfers between devices, body(): table = lax.all_to_all(request, AXES, 0, 0, tiled=True)  9.52 us
    all_to_all x1, waiting for transfers between devices, body(): table = lax.all_to_all(request, AXES, 0, 0, tiled=True)  5.18 us
    all_to_all x1, starting transfers between devices, body(): arrived = lax.all_to_all(send, AXES, 0, 0, tiled=True)  4.6 us
    ppermute x1, starting transfers between devices, shifted(): lax.ppermute(value, axis, [(source, source + steps) for source in range(f...  3.95 us
    unnamed x8, local copies, waits for them, and re-layouts  3.8 us
    pallas_call x1, Pallas kernels, body(): pl.pallas_call(second_kernel, out_shape=(shape(reps, B), shape(devices, B...  3.67 us
  transfers between devices with their start and end apart: 4, of which 1 were waited for; matrix products, arithmetic and copies ran while one was open for 0% of the time, Pallas kernels for 32%

profile of v6, /device:TPU:1, one launch (start us, length us, event | category | flops | bytes accessed | tf_op | source)
XLA Modules:
  0.0 85.2 jit_solution(11603069370181228467)
XLA Ops:
  0.6 2.0 %request_part.1 = (f32[128,128]{1,0:T(8,128)}, f32[536,128]{1,0:T(8,128)}) custom-call(f32[6]{0:T(128)} %theta.1, f32[4,16]{1,0:T(4,128)} %coarse_coords.1, s32[1,384]{1,0:T(1,128)} %coarse.1, f32[4,128]{1,0:T(4,128)} %coords.1, f32[512,128]{1,0:T(8,128)} %values.1, s32[1,128]{1,0:T(1,128)} %fine.1), custom_call_target="tpu_custom_call" | custom-call | tf_op jit(solution)/shard_map/request_part/pallas_call | solution.py:404
  2.6 2.1 %collective-permute-start.1 = (f32[536,128]{1,0:T(8,128)}, f32[536,128]{1,0:T(8,128)S(1)}, u32[]{:S(2)}, u32[]{:S(2)}) collective-permute-start(f32[536,128]{1,0:T(8,128)} %get-tuple-element.7.tile), channel_id=1, source_target_pairs={{15,0},{0,1},{1,2},{2,3},{3,4},{4,5},{5,6},{6,7},{7,8},{8,9},{9,10... | collective-permute-start | bytes 823304 | tf_op jit(solution)/shard_map/ppermute | solution.py:38
  4.8 4.0 %collective-permute-start = (f32[536,128]{1,0:T(8,128)}, f32[536,128]{1,0:T(8,128)S(1)}, u32[]{:S(2)}, u32[]{:S(2)}) collective-permute-start(f32[536,128]{1,0:T(8,128)} %get-tuple-element.7.tile), channel_id=1, source_target_pairs={{0,16},{16,32},{32,48},{48,64},{64,80},{80,96},{96,112},{1,17},{17... | collective-permute-start | bytes 823304 | tf_op jit(solution)/shard_map/ppermute | solution.py:32
  8.7 9.5 %all-to-all-start = ((f32[128,1,128]{2,1,0:T(1,128)}), f32[128,1,128]{2,1,0:T(1,128)S(1)}, u32[]{:S(2)}, u32[]{:S(2)}) async-start(f32[128,1,128]{2,1,0:T(1,128)} %bitcast.17), calls=%async_computation | async-start | bytes 131072 | tf_op jit(solution)/shard_map/all_to_all | solution.py:414
  18.2 0.0 copy-start.2
  18.3 0.0 collective-permute-done.1.left
  18.3 0.0 collective-permute-done.up
  18.3 0.0 copy-start.3
  18.3 0.9 %copy-done.3 = f32[536,128]{1,0:T(8,128)S(1)} copy-done((f32[536,128]{1,0:T(8,128)S(1)}, f32[536,128]{1,0:T(8,128)}, u32[]{:S(2)}) %copy-start.3) | copy-done | bytes 274456
  19.2 3.5 %fine_part.1.after.given.fine = f32[264,640]{1,0:T(8,128)S(1)} custom-call(f32[536,128]{1,0:T(8,128)S(1)} %copy-done.3, f32[536,128]{1,0:T(8,128)S(1)} %collective-permute-done.up, f32[536,128]{1,0:T(8,128)S(1)} %collective-permute-done.1.left), custom_call_target="tpu_custom_call" | custom-call | flops 4000000000 | bytes 1048576 | tf_op jit(solution)/shard_map/fine_part/pallas_call | solution.py:415
  22.8 5.2 %all-to-all-done = f32[128,1,128]{2,1,0:T(1,128)S(1)} async-done(((f32[128,1,128]{2,1,0:T(1,128)}), f32[128,1,128]{2,1,0:T(1,128)S(1)}, u32[]{:S(2)}, u32[]{:S(2)}) %all-to-all-start) | async-done | bytes 65568 | tf_op jit(solution)/shard_map/all_to_all | solution.py:414
  28.0 0.0 copy-done.2
  28.0 1.7 %send_part.1 = f32[3072,128]{1,0:T(8,128)} custom-call(f32[128,128]{1,0:T(8,128)S(1)} %bitcast.12, f32[16,512]{1,0:T(8,128)S(1)} %bitcast.16, f32[264,640]{1,0:T(8,128)S(1)} %fine_part.1.after.given.fine), custom_call_target="tpu_custom_call" | custom-call | tf_op jit(solution)/shard_map/send_part/pallas_call | solution.py:424
  29.6 4.6 %all-to-all-start.1 = ((f32[128,24,128]{2,1,0:T(8,128)}), f32[128,24,128]{2,1,0:T(8,128)S(1)}, u32[]{:S(2)}, u32[]{:S(2)}) async-start(f32[128,24,128]{2,1,0:T(8,128)} %bitcast.4), calls=%async_computation.1 | async-start | bytes 3145728 | tf_op jit(solution)/shard_map/all_to_all | solution.py:432
  34.2 23.7 %fisher_part.1.given = f32[776,640]{1,0:T(8,128)S(1)} custom-call(f32[128,128]{1,0:T(8,128)S(1)} %bitcast.13, f32[264,640]{1,0:T(8,128)S(1)} %fine_part.1.after.given.fine), custom_call_target="tpu_custom_call" | custom-call | flops 30000001024 | bytes 1048576 | tf_op jit(solution)/shard_map/fisher_part/pallas_call | solution.py:433
  58.0 0.0 copy-start
  58.0 1.3 %copy-done = f32[776,640]{1,0:T(8,128)} copy-done((f32[776,640]{1,0:T(8,128)}, f32[776,640]{1,0:T(8,128)S(1)}, u32[]{:S(2)}) %copy-start) | copy-done | bytes 1986584
  59.3 0.0 all-to-all-done.1
  59.3 0.0 copy-start.1
  59.3 1.6 %copy-done.1 = f32[776,640]{1,0:T(8,128)S(1)} copy-done((f32[776,640]{1,0:T(8,128)S(1)}, f32[776,640]{1,0:T(8,128)}, u32[]{:S(2)}) %copy-start.1) | copy-done | bytes 1986584
  60.8 3.7 %gradient_part.1 = (f32[512,128]{1,0:T(8,128)}, f32[128,128]{1,0:T(8,128)S(1)}) custom-call(f32[3072,128]{1,0:T(8,128)S(1)} %bitcast.11, f32[776,640]{1,0:T(8,128)S(1)} %copy-done.1, f32[264,640]{1,0:T(8,128)S(1)} %fine_part.1.after.given.fine), custom_call_target="tpu_custom_call" | custom-call | tf_op jit(solution)/shard_map/gradient_part/pallas_call | solution.py:453
  64.5 19.4 %all_to_all.33 = f32[128,1,128]{2,1,0:T(1,128)S(1)} all-to-all(f32[128,1,128]{2,1,0:T(1,128)S(1)} %bitcast.15), channel_id=1, replica_groups=mesh['row'=8,'col'=16] {'row','col'}, dimensions={0} | all-to-all | bytes 131072 | tf_op jit(solution)/shard_map/all_to_all | solution.py:462
  83.8 1.4 %solve_part.1 = f32[6]{0:T(128)} custom-call(f32[128,128]{1,0:T(8,128)S(1)} %bitcast.14), custom_call_target="tpu_custom_call" | custom-call | tf_op jit(solution)/shard_map/solve_part/pallas_call | solution.py:463
Async XLA Ops:
  2.6 15.6 %collective-permute-start.1 = (f32[536,128]{1,0:T(8,128)}, f32[536,128]{1,0:T(8,128)S(1)}, u32[]{:S(2)}, u32[]{:S(2)}) collective-permute-start(f32[536,128]{1,0:T(8,128)} %get-tuple-element.7.tile), channel_id=1, source_target_pairs={{15,0},{0,1},{1,2},{2,3},{3,4},{4,5},{5,6},{6,7},{7,8},{8,9},{9,10... | collective-permute-start | bytes 823304 | tf_op jit(solution)/shard_map/ppermute | solution.py:38
  4.8 13.5 %collective-permute-start = (f32[536,128]{1,0:T(8,128)}, f32[536,128]{1,0:T(8,128)S(1)}, u32[]{:S(2)}, u32[]{:S(2)}) collective-permute-start(f32[536,128]{1,0:T(8,128)} %get-tuple-element.7.tile), channel_id=1, source_target_pairs={{0,16},{16,32},{32,48},{48,64},{64,80},{80,96},{96,112},{1,17},{17... | collective-permute-start | bytes 823304 | tf_op jit(solution)/shard_map/ppermute | solution.py:32
  8.7 19.2 %all-to-all-start = ((f32[128,1,128]{2,1,0:T(1,128)}), f32[128,1,128]{2,1,0:T(1,128)S(1)}, u32[]{:S(2)}, u32[]{:S(2)}) async-start(f32[128,1,128]{2,1,0:T(1,128)} %bitcast.17), calls=%async_computation | async-start | bytes 131072 | tf_op jit(solution)/shard_map/all_to_all | solution.py:414
  18.2 9.7 %copy-start.2 = (f32[512,16]{0,1:T(8,128)S(1)}, f32[512,16]{0,1:T(8,128)}, u32[]{:S(2)}) copy-start(f32[512,16]{0,1:T(8,128)} %param.10) | copy-start | bytes 98308
  18.3 1.0 %copy-start.3 = (f32[536,128]{1,0:T(8,128)S(1)}, f32[536,128]{1,0:T(8,128)}, u32[]{:S(2)}) copy-start(f32[536,128]{1,0:T(8,128)} %get-tuple-element.7.tile) | copy-start | bytes 823300
  29.6 29.6 %all-to-all-start.1 = ((f32[128,24,128]{2,1,0:T(8,128)}), f32[128,24,128]{2,1,0:T(8,128)S(1)}, u32[]{:S(2)}, u32[]{:S(2)}) async-start(f32[128,24,128]{2,1,0:T(8,128)} %bitcast.4), calls=%async_computation.1 | async-start | bytes 3145728 | tf_op jit(solution)/shard_map/all_to_all | solution.py:432
  58.0 1.3 %copy-start = (f32[776,640]{1,0:T(8,128)}, f32[776,640]{1,0:T(8,128)S(1)}, u32[]{:S(2)}) copy-start(f32[776,640]{1,0:T(8,128)S(1)} %fisher_part.1.given) | copy-start | bytes 5959684
  59.3 1.6 %copy-start.1 = (f32[776,640]{1,0:T(8,128)S(1)}, f32[776,640]{1,0:T(8,128)}, u32[]{:S(2)}) copy-start(f32[776,640]{1,0:T(8,128)} %copy-done) | copy-start | bytes 5959684
